TPU v7x, 512 devices: a whole 4x4x16 slice. The times are simulated.
512 devices in a mesh: gx: 16 (over y, x), depth: 32 (over z, core).
Axes of the slice: x: 4, y: 4, z: 16, core: 2. Of those that a mesh axis runs over, the one named last changes fastest.
Arguments:
- volume: float32 [4, 256, 32, 2048], P(None, 'depth', None, 'gx'), may hold values from -16 to 16
- extinction: float32 [128], replicated, may hold values from 0.05 to 50
- palette: float32 [16, 3], replicated, may hold values from 0.2 to 1.5
- palette_index: int32 [128], replicated, may hold values from 0 to 15
Outputs:
- image: float32 [4, 16, 4096], P(None, 'gx', 'depth')
All inputs are finite; a program needn't handle non-finite values.
Results may differ from a plain program's by a relative error of at most 0.0003.
Values sent between devices are 32-bit elements; how exact they have to be, the bound alone decides.
A program may use at most 64 MiB of HBM per device.

v0:
```python
import jax
import jax.numpy as jnp
import numpy as np
from jax import lax
from jax.sharding import PartitionSpec as P

TAPS = (0.0625, 0.25, 0.375, 0.25, 0.0625)
LIGHT = (0.64, 0.6, 0.48)


def padded_2(array, sides, width):
    for axis, dim in sides:
        size, length = (lax.axis_size(axis), array.shape[dim])
        up = [(i, (i + 1) % size) for i in range(size - 1)]
        down = [(j, i) for i, j in up]
        last = lax.slice_in_dim(array, length - width, length, axis=dim)
        initial = lax.slice_in_dim(array, 0, width, axis=dim)
        before = lax.ppermute(last, axis, up)
        after = lax.ppermute(initial, axis, down)
        array = jnp.concatenate([before, array, after], axis=dim)
    return array


def swapped(array, axis, distance):
    return lax.ppermute(array, axis, [(i, i ^ 1 << distance) for i in range(lax.axis_size(axis))])


def smooth_valid(values, along):
    length = values.shape[along] - 4
    result = TAPS[0] * lax.slice_in_dim(values, 0, length, axis=along)
    for offset in range(1, 5):
        result = result + TAPS[offset] * lax.slice_in_dim(
            values, offset, offset + length, axis=along
        )
    return result


def smooth_zero(values, along):
    widths = [(0, 0)] * values.ndim
    widths[along] = (2, 2)
    return smooth_valid(jnp.pad(values, widths), along)


def gradients(fields):
    centre = fields[:, 1:-1, :, 1:-1]
    grad_z = 0.5 * (fields[:, 2:, :, 1:-1] - fields[:, :-2, :, 1:-1])
    grad_x = 0.5 * (fields[:, 1:-1, :, 2:] - fields[:, 1:-1, :, :-2])
    padded = jnp.pad(centre, ((0, 0), (0, 0), (1, 1), (0, 0)))
    grad_y = 0.5 * (padded[:, :, 2:] - padded[:, :, :-2])
    return (grad_z, grad_y, grad_x)


def table_lookup(tables, position):
    entries = tables.shape[1]
    stops = jnp.arange(entries, dtype=position.dtype)

    def one_layer(layer):
        hats = jnp.maximum(0.0, 1.0 - jnp.abs(layer[None, :, :] - stops[:, None, None]))
        return jnp.einsum("tk,kyx->tyx", tables, hats, precision=lax.Precision.HIGHEST)

    stacked = lax.map(one_layer, position)
    return jnp.moveaxis(stacked, 1, 0)


def emission_terms(centre, fields, extinction, colors, step_len):
    grad_z, grad_y, grad_x = gradients(fields)
    facing = LIGHT[0] * grad_z[0] + LIGHT[1] * grad_y[0] + LIGHT[2] * grad_x[0]
    slope_dens = grad_z[0] * grad_z[0] + grad_y[0] * grad_y[0] + grad_x[0] * grad_x[0]
    shading = 0.35 + 0.65 * facing * facing / (slope_dens + 0.05)
    slope_temp = grad_z[1] * grad_z[1] + grad_y[1] * grad_y[1] + grad_x[1] * grad_x[1]
    opacity_gain = 0.25 + 1.5 * slope_temp / (slope_temp + 0.1)
    entries = extinction.shape[0]
    position = (entries - 1) * jax.nn.sigmoid(2.0 * centre[0])
    tables = jnp.concatenate([extinction[None, :], colors.T], axis=0)
    looked = table_lookup(tables, position)
    optical = looked[0] * opacity_gain * step_len
    brighten = (1.0 + 0.5 * jnp.tanh(centre[2])) * jnp.exp(0.5 * jnp.tanh(centre[3])) * shading
    emission = looked[1:] * brighten
    return (optical, emission)


def composite(optical, emission):
    running = jnp.cumsum(optical, axis=0)
    weight = jnp.exp(optical - running) * -jnp.expm1(-optical)
    color = jnp.sum(weight[None] * emission, axis=1)
    through = jnp.exp(-running[-1])
    return (color, through)


def over(nearer, farther):
    return jnp.concatenate(
        [nearer[:3] + nearer[3:4] * farther[:3], nearer[3:4] * farther[3:4]], axis=0
    )


def reverse_bits(place, rounds):
    flipped = 0
    for level in range(rounds):
        flipped = flipped * 2 + (place >> level & 1)
    return flipped


def per_device(volume, extinction, palette, palette_index):
    depth_devs = lax.axis_size("depth")
    depth_cells = volume.shape[1]
    height = volume.shape[2]
    x_count = volume.shape[3]
    padded = padded_2(volume, (("gx", 3), ("depth", 1)), 2)
    centre = smooth_valid(smooth_zero(smooth_valid(padded, 1), 2), 3)
    fields = padded_2(centre[:2], (("gx", 3), ("depth", 1)), 1)
    onehot = (
        palette_index[:, None] == jnp.arange(palette.shape[0], dtype=jnp.int32)[None, :]
    ).astype(jnp.float32)
    colors = jnp.dot(onehot, palette, precision=lax.Precision.HIGHEST)
    step_len = 0.25 / (depth_cells * depth_devs)
    optical, emission = emission_terms(centre, fields, extinction, colors, step_len)
    color, through = composite(optical, emission)
    pixels = height * x_count
    partial_value = jnp.concatenate([color.reshape(3, pixels), through.reshape(1, pixels)], axis=0)
    piece_len = pixels // depth_devs
    rounds = depth_devs.bit_length() - 1
    reorder = np.array([reverse_bits(place, rounds) for place in range(depth_devs)], dtype=np.int32)
    current = partial_value.reshape(4, depth_devs, piece_len)[:, reorder, :].reshape(4, pixels)
    my_index = lax.axis_index("depth")
    for bit_number in range(rounds):
        halfway = current.shape[1] // 2
        lower = current[:, :halfway]
        higher = current[:, halfway:]
        upper = my_index // 2**bit_number % 2 == 1
        retained = jnp.where(upper, higher, lower)
        outgoing = jnp.where(upper, lower, higher)
        received = swapped(outgoing, "depth", bit_number)
        current = jnp.where(upper, over(received, retained), over(retained, received))
    result = jnp.concatenate([current[:3], 1.0 - current[3:4]], axis=0)
    return result.reshape(4, 1, piece_len)


def solution(mesh):
    placed = (P(None, "depth", None, "gx"), P(), P(), P())
    return jax.shard_map(
        per_device, mesh=mesh, in_specs=placed, out_specs=P(None, "gx", "depth"), check_vma=False
    )
```

profile of v0, /device:TPU:38, one launch (start us, length us, event | category | flops | bytes accessed | tf_op | source)
XLA Modules:
  0.0 124.6 jit_solution(7964660236160628884)
XLA Ops:
  0.0 1.4 %copy.17 = f32[4,8,32,128]{3,1,2,0:T(8,128)S(1)} copy(f32[4,8,32,128]{3,2,1,0:T(8,128)} %param.8) | data formatting | bytes 1048576 | tf_op args[0]
  1.6 3.5 %collective-permute-start = (f32[4,8,32,2]{3,1,2,0:T(8,128)S(1)}, f32[4,8,32,2]{3,1,2,0:T(8,128)S(1)}, u32[]{:S(2)}, u32[]{:S(2)}) collective-permute-start(f32[4,8,32,2]{3,1,2,0:T(8,128)S(1)} %get-tuple-element.71), channel_id=1, source_target_pairs={{0,32},{32,64},{64,96},{96,128},{128,160},{160,192},{192,224},{224... | collective-permute-start | bytes 24584 | tf_op jit(solution)/shard_map/ppermute | solution.py:18
  5.1 2.4 %collective-permute-start.1 = (f32[4,8,32,2]{3,1,2,0:T(8,128)S(1)}, f32[4,8,32,2]{3,1,2,0:T(8,128)S(1)}, u32[]{:S(2)}, u32[]{:S(2)}) collective-permute-start(f32[4,8,32,2]{3,1,2,0:T(8,128)S(1)} %get-tuple-element.72), channel_id=1, source_target_pairs={{32,0},{64,32},{96,64},{128,96},{160,128},{192,160},{224,192},{256... | collective-permute-start | bytes 24584 | tf_op jit(solution)/shard_map/ppermute | solution.py:19
  7.8 9.5 %collective-permute-done = f32[4,8,32,2]{3,1,2,0:T(8,128)S(1)} collective-permute-done((f32[4,8,32,2]{3,1,2,0:T(8,128)S(1)}, f32[4,8,32,2]{3,1,2,0:T(8,128)S(1)}, u32[]{:S(2)}, u32[]{:S(2)}) %collective-permute-start) | collective-permute-done | bytes 8224 | tf_op jit(solution)/shard_map/ppermute | solution.py:18
  17.3 5.2 %collective-permute-done.1 = f32[4,8,32,2]{3,1,2,0:T(8,128)S(1)} collective-permute-done((f32[4,8,32,2]{3,1,2,0:T(8,128)S(1)}, f32[4,8,32,2]{3,1,2,0:T(8,128)S(1)}, u32[]{:S(2)}, u32[]{:S(2)}) %collective-permute-start.1) | collective-permute-done | bytes 8224 | tf_op jit(solution)/shard_map/ppermute | solution.py:19
  23.2 1.9 %collective-permute-start.2 = (f32[4,2,32,132]{3,1,2,0:T(2,128)S(1)}, f32[4,2,32,132]{3,1,2,0:T(2,128)S(1)}, u32[]{:S(2)}, u32[]{:S(2)}) collective-permute-start(f32[4,2,32,132]{3,1,2,0:T(2,128)S(1)} %get-tuple-element.61), channel_id=1, source_target_pairs={{0,1},{1,2},{2,3},{3,4},{4,5},{5,6},{6,7},{7,8},{8,9},{9,10},{10,1... | collective-permute-start | bytes 405512 | tf_op jit(solution)/shard_map/ppermute | solution.py:18
  25.1 3.6 %collective-permute-start.3 = (f32[4,2,32,132]{3,1,2,0:T(2,128)S(1)}, f32[4,2,32,132]{3,1,2,0:T(2,128)S(1)}, u32[]{:S(2)}, u32[]{:S(2)}) collective-permute-start(f32[4,2,32,132]{3,1,2,0:T(2,128)S(1)} %get-tuple-element.62), channel_id=1, source_target_pairs={{1,0},{2,1},{3,2},{4,3},{5,4},{6,5},{7,6},{8,7},{9,8},{10,9},{11,1... | collective-permute-start | bytes 405512 | tf_op jit(solution)/shard_map/ppermute | solution.py:19
  28.8 2.0 %collective-permute-done.2 = f32[4,2,32,132]{3,1,2,0:T(2,128)S(1)} collective-permute-done((f32[4,2,32,132]{3,1,2,0:T(2,128)S(1)}, f32[4,2,32,132]{3,1,2,0:T(2,128)S(1)}, u32[]{:S(2)}, u32[]{:S(2)}) %collective-permute-start.2) | collective-permute-done | bytes 135200 | tf_op jit(solution)/shard_map/ppermute | solution.py:18
  30.9 1.8 %collective-permute-done.3 = f32[4,2,32,132]{3,1,2,0:T(2,128)S(1)} collective-permute-done((f32[4,2,32,132]{3,1,2,0:T(2,128)S(1)}, f32[4,2,32,132]{3,1,2,0:T(2,128)S(1)}, u32[]{:S(2)}, u32[]{:S(2)}) %collective-permute-start.3) | collective-permute-done | bytes 135200 | tf_op jit(solution)/shard_map/ppermute | solution.py:19
  32.6 1.4 %maximum_maximum_fusion = (f32[4,10,32,132]{3,1,2,0:T(8,128)S(1)}, f32[4,10,32,132]{3,1,2,0:T(8,128)S(1)}) fusion(f32[4,8,32,2]{3,1,2,0:T(8,128)S(1)} %collective-permute-done.1, f32[4,8,32,128]{3,1,2,0:T(8,128)S(1)} %copy.17, f32[4,8,32,2]{3,1,2,0:T(8,128)S(1)} %collective-permute-done, f32[4,2,32,132]{3,1,2,0:T(2,128)S(1)} %collective-permute-done.2, ...), kind=kLoop, calls=%fused_computation.15 | loop fusion | flops 1013760 | bytes 2162688 | tf_op jit(solution)/shard_map/concatenate | solution.py:20
  34.0 0.7 fusion.24
  35.0 0.6 fusion.28
  35.7 1.9 %collective-permute-start.4 = (f32[2,8,32,1]{3,1,2,0:T(8,128)S(1)}, f32[2,8,32,1]{3,1,2,0:T(8,128)S(1)}, u32[]{:S(2)}, u32[]{:S(2)}) collective-permute-start(f32[2,8,32,1]{3,1,2,0:T(8,128)S(1)} %get-tuple-element.70), channel_id=1, source_target_pairs={{0,32},{32,64},{64,96},{96,128},{128,160},{160,192},{192,224},{224... | collective-permute-start | bytes 6152 | tf_op jit(solution)/shard_map/ppermute | solution.py:18
  37.6 3.9 %collective-permute-start.5 = (f32[2,8,32,1]{3,1,2,0:T(8,128)S(1)}, f32[2,8,32,1]{3,1,2,0:T(8,128)S(1)}, u32[]{:S(2)}, u32[]{:S(2)}) collective-permute-start(f32[2,8,32,1]{3,1,2,0:T(8,128)S(1)} %get-tuple-element.69), channel_id=1, source_target_pairs={{32,0},{64,32},{96,64},{128,96},{160,128},{192,160},{224,192},{256... | collective-permute-start | bytes 6152 | tf_op jit(solution)/shard_map/ppermute | solution.py:19
  41.6 3.9 %collective-permute-done.4 = f32[2,8,32,1]{3,1,2,0:T(8,128)S(1)} collective-permute-done((f32[2,8,32,1]{3,1,2,0:T(8,128)S(1)}, f32[2,8,32,1]{3,1,2,0:T(8,128)S(1)}, u32[]{:S(2)}, u32[]{:S(2)}) %collective-permute-start.4) | collective-permute-done | bytes 2080 | tf_op jit(solution)/shard_map/ppermute | solution.py:18
  45.5 4.0 %collective-permute-done.5 = f32[2,8,32,1]{3,1,2,0:T(8,128)S(1)} collective-permute-done((f32[2,8,32,1]{3,1,2,0:T(8,128)S(1)}, f32[2,8,32,1]{3,1,2,0:T(8,128)S(1)}, u32[]{:S(2)}, u32[]{:S(2)}) %collective-permute-start.5) | collective-permute-done | bytes 2080 | tf_op jit(solution)/shard_map/ppermute | solution.py:19
  50.0 1.9 %collective-permute-start.6 = (f32[2,1,32,130]{3,1,2,0:T(1,128)S(1)}, f32[2,1,32,130]{3,1,2,0:T(1,128)S(1)}, u32[]{:S(2)}, u32[]{:S(2)}) collective-permute-start(f32[2,1,32,130]{3,1,2,0:T(1,128)S(1)} %get-tuple-element.67), channel_id=1, source_target_pairs={{1,0},{2,1},{3,2},{4,3},{5,4},{6,5},{7,6},{8,7},{9,8},{10,9},{11,1... | collective-permute-start | bytes 99848 | tf_op jit(solution)/shard_map/ppermute | solution.py:19
  52.0 3.0 %collective-permute-start.7 = (f32[2,1,32,130]{3,1,2,0:T(1,128)S(1)}, f32[2,1,32,130]{3,1,2,0:T(1,128)S(1)}, u32[]{:S(2)}, u32[]{:S(2)}) collective-permute-start(f32[2,1,32,130]{3,1,2,0:T(1,128)S(1)} %get-tuple-element.68), channel_id=1, source_target_pairs={{0,1},{1,2},{2,3},{3,4},{4,5},{5,6},{6,7},{7,8},{8,9},{9,10},{10,1... | collective-permute-start | bytes 99848 | tf_op jit(solution)/shard_map/ppermute | solution.py:18
  55.0 23.1 %while.11 = (s32[]{:T(128)}, f32[8,4,32,128]{3,0,2,1:T(8,128)S(1)}, f32[8,32,128]{2,0,1:T(8,128)S(1)}, f32[4,128]{1,0:T(4,128)S(1)}, s32[]{:T(128)}, /*index=5*/s32[]{:T(128)}) while((s32[]{:T(128)}, f32[8,4,32,128]{3,0,2,1:T(8,128)S(1)}, f32[8,32,128]{2,0,1:T(8,128)S(1)}, f32[4,128]{1,0:T(4,128)S(1)}, s32[]{:T(128)}, ...), condition=%wide.region_1.2_spmd.clone, body=%wide.region_0.1_spmd.clone.sunk | while | flops 27262976 | bytes 378957 | solution.py:61
  55.0 1.5 %fusion.81 = f32[1,4,32,128]{3,1,2,0:T(4,128)S(1)} fusion(f32[32,128]{1,0:T(8,128)S(1)} %bitcast.56, f32[4,128]{1,0:T(4,128)S(1)} %get-tuple-element.149), kind=kOutput, calls=%fused_computation.7.clone.1 | convolution fusion | flops 27262976 | bytes 83968 | tf_op jit(solution)/shard_map/while/body/eval_jaxpr/tk,kyx->tyx/dot_general | solution.py:59
  56.5 1.3 %dynamic_update_slice.6 = f32[8,4,32,128]{3,0,2,1:T(8,128)S(1)} dynamic-update-slice(f32[8,4,32,128]{3,0,2,1:T(8,128)S(1)} %get-tuple-element.141, f32[1,4,32,128]{3,0,2,1:T(1,128)S(1)} %copy.31, s32[]{:T(128)} %get-tuple-element.140, s32[]{:T(128)} %constant.124.clone.1..sunk, s32[]{:T(128)} %constant.124.clone.1..sunk, s32[]{:T(128)} %constant.124.clone.1..sunk) | dynamic-update-slice | bytes 131076 | tf_op jit(solution)/shard_map/while/body/jit(dynamic_update_index_in_dim)/dynamic_update_slice | solution.py:61
  57.9 1.5 %fusion.81 = f32[1,4,32,128]{3,1,2,0:T(4,128)S(1)} fusion(f32[32,128]{1,0:T(8,128)S(1)} %bitcast.56, f32[4,128]{1,0:T(4,128)S(1)} %get-tuple-element.149), kind=kOutput, calls=%fused_computation.7.clone.1 | convolution fusion | flops 27262976 | bytes 83968 | tf_op jit(solution)/shard_map/while/body/eval_jaxpr/tk,kyx->tyx/dot_general | solution.py:59
  59.4 1.3 %dynamic_update_slice.6 = f32[8,4,32,128]{3,0,2,1:T(8,128)S(1)} dynamic-update-slice(f32[8,4,32,128]{3,0,2,1:T(8,128)S(1)} %get-tuple-element.141, f32[1,4,32,128]{3,0,2,1:T(1,128)S(1)} %copy.31, s32[]{:T(128)} %get-tuple-element.140, s32[]{:T(128)} %constant.124.clone.1..sunk, s32[]{:T(128)} %constant.124.clone.1..sunk, s32[]{:T(128)} %constant.124.clone.1..sunk) | dynamic-update-slice | bytes 131076 | tf_op jit(solution)/shard_map/while/body/jit(dynamic_update_index_in_dim)/dynamic_update_slice | solution.py:61
  60.8 1.5 %fusion.81 = f32[1,4,32,128]{3,1,2,0:T(4,128)S(1)} fusion(f32[32,128]{1,0:T(8,128)S(1)} %bitcast.56, f32[4,128]{1,0:T(4,128)S(1)} %get-tuple-element.149), kind=kOutput, calls=%fused_computation.7.clone.1 | convolution fusion | flops 27262976 | bytes 83968 | tf_op jit(solution)/shard_map/while/body/eval_jaxpr/tk,kyx->tyx/dot_general | solution.py:59
  62.3 1.3 %dynamic_update_slice.6 = f32[8,4,32,128]{3,0,2,1:T(8,128)S(1)} dynamic-update-slice(f32[8,4,32,128]{3,0,2,1:T(8,128)S(1)} %get-tuple-element.141, f32[1,4,32,128]{3,0,2,1:T(1,128)S(1)} %copy.31, s32[]{:T(128)} %get-tuple-element.140, s32[]{:T(128)} %constant.124.clone.1..sunk, s32[]{:T(128)} %constant.124.clone.1..sunk, s32[]{:T(128)} %constant.124.clone.1..sunk) | dynamic-update-slice | bytes 131076 | tf_op jit(solution)/shard_map/while/body/jit(dynamic_update_index_in_dim)/dynamic_update_slice | solution.py:61
  63.7 1.5 %fusion.81 = f32[1,4,32,128]{3,1,2,0:T(4,128)S(1)} fusion(f32[32,128]{1,0:T(8,128)S(1)} %bitcast.56, f32[4,128]{1,0:T(4,128)S(1)} %get-tuple-element.149), kind=kOutput, calls=%fused_computation.7.clone.1 | convolution fusion | flops 27262976 | bytes 83968 | tf_op jit(solution)/shard_map/while/body/eval_jaxpr/tk,kyx->tyx/dot_general | solution.py:59
  65.2 1.3 %dynamic_update_slice.6 = f32[8,4,32,128]{3,0,2,1:T(8,128)S(1)} dynamic-update-slice(f32[8,4,32,128]{3,0,2,1:T(8,128)S(1)} %get-tuple-element.141, f32[1,4,32,128]{3,0,2,1:T(1,128)S(1)} %copy.31, s32[]{:T(128)} %get-tuple-element.140, s32[]{:T(128)} %constant.124.clone.1..sunk, s32[]{:T(128)} %constant.124.clone.1..sunk, s32[]{:T(128)} %constant.124.clone.1..sunk) | dynamic-update-slice | bytes 131076 | tf_op jit(solution)/shard_map/while/body/jit(dynamic_update_index_in_dim)/dynamic_update_slice | solution.py:61
  66.5 1.5 %fusion.81 = f32[1,4,32,128]{3,1,2,0:T(4,128)S(1)} fusion(f32[32,128]{1,0:T(8,128)S(1)} %bitcast.56, f32[4,128]{1,0:T(4,128)S(1)} %get-tuple-element.149), kind=kOutput, calls=%fused_computation.7.clone.1 | convolution fusion | flops 27262976 | bytes 83968 | tf_op jit(solution)/shard_map/while/body/eval_jaxpr/tk,kyx->tyx/dot_general | solution.py:59
  68.1 1.3 %dynamic_update_slice.6 = f32[8,4,32,128]{3,0,2,1:T(8,128)S(1)} dynamic-update-slice(f32[8,4,32,128]{3,0,2,1:T(8,128)S(1)} %get-tuple-element.141, f32[1,4,32,128]{3,0,2,1:T(1,128)S(1)} %copy.31, s32[]{:T(128)} %get-tuple-element.140, s32[]{:T(128)} %constant.124.clone.1..sunk, s32[]{:T(128)} %constant.124.clone.1..sunk, s32[]{:T(128)} %constant.124.clone.1..sunk) | dynamic-update-slice | bytes 131076 | tf_op jit(solution)/shard_map/while/body/jit(dynamic_update_index_in_dim)/dynamic_update_slice | solution.py:61
  69.4 1.5 %fusion.81 = f32[1,4,32,128]{3,1,2,0:T(4,128)S(1)} fusion(f32[32,128]{1,0:T(8,128)S(1)} %bitcast.56, f32[4,128]{1,0:T(4,128)S(1)} %get-tuple-element.149), kind=kOutput, calls=%fused_computation.7.clone.1 | convolution fusion | flops 27262976 | bytes 83968 | tf_op jit(solution)/shard_map/while/body/eval_jaxpr/tk,kyx->tyx/dot_general | solution.py:59
  71.0 1.3 %dynamic_update_slice.6 = f32[8,4,32,128]{3,0,2,1:T(8,128)S(1)} dynamic-update-slice(f32[8,4,32,128]{3,0,2,1:T(8,128)S(1)} %get-tuple-element.141, f32[1,4,32,128]{3,0,2,1:T(1,128)S(1)} %copy.31, s32[]{:T(128)} %get-tuple-element.140, s32[]{:T(128)} %constant.124.clone.1..sunk, s32[]{:T(128)} %constant.124.clone.1..sunk, s32[]{:T(128)} %constant.124.clone.1..sunk) | dynamic-update-slice | bytes 131076 | tf_op jit(solution)/shard_map/while/body/jit(dynamic_update_index_in_dim)/dynamic_update_slice | solution.py:61
  72.3 1.5 %fusion.81 = f32[1,4,32,128]{3,1,2,0:T(4,128)S(1)} fusion(f32[32,128]{1,0:T(8,128)S(1)} %bitcast.56, f32[4,128]{1,0:T(4,128)S(1)} %get-tuple-element.149), kind=kOutput, calls=%fused_computation.7.clone.1 | convolution fusion | flops 27262976 | bytes 83968 | tf_op jit(solution)/shard_map/while/body/eval_jaxpr/tk,kyx->tyx/dot_general | solution.py:59
  73.9 1.3 %dynamic_update_slice.6 = f32[8,4,32,128]{3,0,2,1:T(8,128)S(1)} dynamic-update-slice(f32[8,4,32,128]{3,0,2,1:T(8,128)S(1)} %get-tuple-element.141, f32[1,4,32,128]{3,0,2,1:T(1,128)S(1)} %copy.31, s32[]{:T(128)} %get-tuple-element.140, s32[]{:T(128)} %constant.124.clone.1..sunk, s32[]{:T(128)} %constant.124.clone.1..sunk, s32[]{:T(128)} %constant.124.clone.1..sunk) | dynamic-update-slice | bytes 131076 | tf_op jit(solution)/shard_map/while/body/jit(dynamic_update_index_in_dim)/dynamic_update_slice | solution.py:61
  75.2 1.5 %fusion.81 = f32[1,4,32,128]{3,1,2,0:T(4,128)S(1)} fusion(f32[32,128]{1,0:T(8,128)S(1)} %bitcast.56, f32[4,128]{1,0:T(4,128)S(1)} %get-tuple-element.149), kind=kOutput, calls=%fused_computation.7.clone.1 | convolution fusion | flops 27262976 | bytes 83968 | tf_op jit(solution)/shard_map/while/body/eval_jaxpr/tk,kyx->tyx/dot_general | solution.py:59
  76.7 1.3 %dynamic_update_slice.6 = f32[8,4,32,128]{3,0,2,1:T(8,128)S(1)} dynamic-update-slice(f32[8,4,32,128]{3,0,2,1:T(8,128)S(1)} %get-tuple-element.141, f32[1,4,32,128]{3,0,2,1:T(1,128)S(1)} %copy.31, s32[]{:T(128)} %get-tuple-element.140, s32[]{:T(128)} %constant.124.clone.1..sunk, s32[]{:T(128)} %constant.124.clone.1..sunk, s32[]{:T(128)} %constant.124.clone.1..sunk) | dynamic-update-slice | bytes 131076 | tf_op jit(solution)/shard_map/while/body/jit(dynamic_update_index_in_dim)/dynamic_update_slice | solution.py:61
  78.1 0.5 fusion.39
  79.3 0.6 gather_fusion
  79.9 3.6 %collective-permute-start.8 = (f32[4,2048]{1,0:T(4,128)S(1)}, f32[4,2048]{1,0:T(4,128)S(1)}, u32[]{:S(2)}, u32[]{:S(2)}) collective-permute-start(f32[4,2048]{1,0:T(4,128)S(1)} %get-tuple-element.76), channel_id=1, source_target_pairs={{0,1},{1,0},{2,3},{3,2},{4,5},{5,4},{6,7},{7,6},{8,9},{9,8},{10,11... | collective-permute-start | bytes 98312 | tf_op jit(solution)/shard_map/ppermute | solution.py:25
  83.6 0.8 collective-permute-done.8
  84.5 1.9 %collective-permute-start.9 = (f32[4,1024]{1,0:T(4,128)S(1)}, f32[4,1024]{1,0:T(4,128)S(1)}, u32[]{:S(2)}, u32[]{:S(2)}) collective-permute-start(f32[4,1024]{1,0:T(4,128)S(1)} %get-tuple-element.80), channel_id=1, source_target_pairs={{0,2},{1,3},{2,0},{3,1},{4,6},{5,7},{6,4},{7,5},{8,10},{9,11},{10,... | collective-permute-start | bytes 49160 | tf_op jit(solution)/shard_map/ppermute | solution.py:25
  86.5 3.7 %collective-permute-done.9 = f32[4,1024]{1,0:T(4,128)S(1)} collective-permute-done((f32[4,1024]{1,0:T(4,128)S(1)}, f32[4,1024]{1,0:T(4,128)S(1)}, u32[]{:S(2)}, u32[]{:S(2)}) %collective-permute-start.9) | collective-permute-done | bytes 16416 | tf_op jit(solution)/shard_map/ppermute | solution.py:25
  90.2 8.1 %collective-permute-start.10 = (f32[4,512]{1,0:T(4,128)S(1)}, f32[4,512]{1,0:T(4,128)S(1)}, u32[]{:S(2)}, u32[]{:S(2)}) collective-permute-start(f32[4,512]{1,0:T(4,128)S(1)} %get-tuple-element.87), channel_id=1, source_target_pairs={{0,4},{1,5},{2,6},{3,7},{4,0},{5,1},{6,2},{7,3},{8,12},{9,13},{10,... | collective-permute-start | bytes 24584 | tf_op jit(solution)/shard_map/ppermute | solution.py:25
  98.3 1.6 %collective-permute-done.10 = f32[4,512]{1,0:T(4,128)S(1)} collective-permute-done((f32[4,512]{1,0:T(4,128)S(1)}, f32[4,512]{1,0:T(4,128)S(1)}, u32[]{:S(2)}, u32[]{:S(2)}) %collective-permute-start.10) | collective-permute-done | bytes 8224 | tf_op jit(solution)/shard_map/ppermute | solution.py:25
  99.9 8.3 %collective-permute-start.11 = (f32[4,256]{1,0:T(4,128)S(1)}, f32[4,256]{1,0:T(4,128)S(1)}, u32[]{:S(2)}, u32[]{:S(2)}) collective-permute-start(f32[4,256]{1,0:T(4,128)S(1)} %get-tuple-element.94), channel_id=1, source_target_pairs={{0,8},{1,9},{2,10},{3,11},{4,12},{5,13},{6,14},{7,15},{8,0},{9,1},... | collective-permute-start | bytes 12296 | tf_op jit(solution)/shard_map/ppermute | solution.py:25
  108.2 1.5 %collective-permute-done.11 = f32[4,256]{1,0:T(4,128)S(1)} collective-permute-done((f32[4,256]{1,0:T(4,128)S(1)}, f32[4,256]{1,0:T(4,128)S(1)}, u32[]{:S(2)}, u32[]{:S(2)}) %collective-permute-start.11) | collective-permute-done | bytes 4128 | tf_op jit(solution)/shard_map/ppermute | solution.py:25
  109.8 11.2 %collective-permute-start.12 = (f32[4,128]{1,0:T(4,128)S(1)}, f32[4,128]{1,0:T(4,128)S(1)}, u32[]{:S(2)}, u32[]{:S(2)}) collective-permute-start(f32[4,128]{1,0:T(4,128)S(1)} %get-tuple-element.101), channel_id=1, source_target_pairs={{0,16},{1,17},{2,18},{3,19},{4,20},{5,21},{6,22},{7,23},{8,24},{9,... | collective-permute-start | bytes 6152 | tf_op jit(solution)/shard_map/ppermute | solution.py:25
  121.0 3.0 %collective-permute-done.12 = f32[4,128]{1,0:T(4,128)S(1)} collective-permute-done((f32[4,128]{1,0:T(4,128)S(1)}, f32[4,128]{1,0:T(4,128)S(1)}, u32[]{:S(2)}, u32[]{:S(2)}) %collective-permute-start.12) | collective-permute-done | bytes 2080 | tf_op jit(solution)/shard_map/ppermute | solution.py:25
  124.1 0.6 pad_maximum_fusion.25
  (66 shorter events, 3.5 us)
Async XLA Ops:
  0.0 7.6 %copy-start = (f32[16,3]{0,1:T(4,128)S(1)}, f32[16,3]{0,1:T(4,128)}, u32[]{:S(2)}) copy-start(f32[16,3]{0,1:T(4,128)} %param.10) | copy-start | bytes 580
  0.0 7.6 %copy-start.3 = (s32[128]{0:T(128)S(1)}, s32[128]{0:T(128)}, u32[]{:S(2)}) copy-start(s32[128]{0:T(128)} %param.11) | copy-start | bytes 1540
  1.6 27.2 %copy-start.1 = (f32[128]{0:T(128)S(1)}, f32[128]{0:T(128)}, u32[]{:S(2)}) copy-start(f32[128]{0:T(128)} %param.9) | copy-start | bytes 1540
  1.6 27.2 %copy-start.2 = (s32[32]{0:T(128)S(1)}, s32[32]{0:T(128)}, u32[]{:S(2)}) copy-start(s32[32]{0:T(128)} %constant.157) | copy-start | bytes 388
  1.6 15.7 %collective-permute-start = (f32[4,8,32,2]{3,1,2,0:T(8,128)S(1)}, f32[4,8,32,2]{3,1,2,0:T(8,128)S(1)}, u32[]{:S(2)}, u32[]{:S(2)}) collective-permute-start(f32[4,8,32,2]{3,1,2,0:T(8,128)S(1)} %get-tuple-element.71), channel_id=1, source_target_pairs={{0,32},{32,64},{64,96},{96,128},{128,160},{160,192},{192,224},{224... | collective-permute-start | bytes 24584 | tf_op jit(solution)/shard_map/ppermute | solution.py:18
  5.1 17.4 %collective-permute-start.1 = (f32[4,8,32,2]{3,1,2,0:T(8,128)S(1)}, f32[4,8,32,2]{3,1,2,0:T(8,128)S(1)}, u32[]{:S(2)}, u32[]{:S(2)}) collective-permute-start(f32[4,8,32,2]{3,1,2,0:T(8,128)S(1)} %get-tuple-element.72), channel_id=1, source_target_pairs={{32,0},{64,32},{96,64},{128,96},{160,128},{192,160},{224,192},{256... | collective-permute-start | bytes 24584 | tf_op jit(solution)/shard_map/ppermute | solution.py:19
  23.2 7.7 %collective-permute-start.2 = (f32[4,2,32,132]{3,1,2,0:T(2,128)S(1)}, f32[4,2,32,132]{3,1,2,0:T(2,128)S(1)}, u32[]{:S(2)}, u32[]{:S(2)}) collective-permute-start(f32[4,2,32,132]{3,1,2,0:T(2,128)S(1)} %get-tuple-element.61), channel_id=1, source_target_pairs={{0,1},{1,2},{2,3},{3,4},{4,5},{5,6},{6,7},{7,8},{8,9},{9,10},{10,1... | collective-permute-start | bytes 405512 | tf_op jit(solution)/shard_map/ppermute | solution.py:18
  25.1 7.5 %collective-permute-start.3 = (f32[4,2,32,132]{3,1,2,0:T(2,128)S(1)}, f32[4,2,32,132]{3,1,2,0:T(2,128)S(1)}, u32[]{:S(2)}, u32[]{:S(2)}) collective-permute-start(f32[4,2,32,132]{3,1,2,0:T(2,128)S(1)} %get-tuple-element.62), channel_id=1, source_target_pairs={{1,0},{2,1},{3,2},{4,3},{5,4},{6,5},{7,6},{8,7},{9,8},{10,9},{11,1... | collective-permute-start | bytes 405512 | tf_op jit(solution)/shard_map/ppermute | solution.py:19
  35.7 9.8 %collective-permute-start.4 = (f32[2,8,32,1]{3,1,2,0:T(8,128)S(1)}, f32[2,8,32,1]{3,1,2,0:T(8,128)S(1)}, u32[]{:S(2)}, u32[]{:S(2)}) collective-permute-start(f32[2,8,32,1]{3,1,2,0:T(8,128)S(1)} %get-tuple-element.70), channel_id=1, source_target_pairs={{0,32},{32,64},{64,96},{96,128},{128,160},{160,192},{192,224},{224... | collective-permute-start | bytes 6152 | tf_op jit(solution)/shard_map/ppermute | solution.py:18
  37.6 11.9 %collective-permute-start.5 = (f32[2,8,32,1]{3,1,2,0:T(8,128)S(1)}, f32[2,8,32,1]{3,1,2,0:T(8,128)S(1)}, u32[]{:S(2)}, u32[]{:S(2)}) collective-permute-start(f32[2,8,32,1]{3,1,2,0:T(8,128)S(1)} %get-tuple-element.69), channel_id=1, source_target_pairs={{32,0},{64,32},{96,64},{128,96},{160,128},{192,160},{224,192},{256... | collective-permute-start | bytes 6152 | tf_op jit(solution)/shard_map/ppermute | solution.py:19
  50.0 28.0 %collective-permute-start.6 = (f32[2,1,32,130]{3,1,2,0:T(1,128)S(1)}, f32[2,1,32,130]{3,1,2,0:T(1,128)S(1)}, u32[]{:S(2)}, u32[]{:S(2)}) collective-permute-start(f32[2,1,32,130]{3,1,2,0:T(1,128)S(1)} %get-tuple-element.67), channel_id=1, source_target_pairs={{1,0},{2,1},{3,2},{4,3},{5,4},{6,5},{7,6},{8,7},{9,8},{10,9},{11,1... | collective-permute-start | bytes 99848 | tf_op jit(solution)/shard_map/ppermute | solution.py:19
  52.0 26.1 %collective-permute-start.7 = (f32[2,1,32,130]{3,1,2,0:T(1,128)S(1)}, f32[2,1,32,130]{3,1,2,0:T(1,128)S(1)}, u32[]{:S(2)}, u32[]{:S(2)}) collective-permute-start(f32[2,1,32,130]{3,1,2,0:T(1,128)S(1)} %get-tuple-element.68), channel_id=1, source_target_pairs={{0,1},{1,2},{2,3},{3,4},{4,5},{5,6},{6,7},{7,8},{8,9},{9,10},{10,1... | collective-permute-start | bytes 99848 | tf_op jit(solution)/shard_map/ppermute | solution.py:18
  79.9 4.5 %collective-permute-start.8 = (f32[4,2048]{1,0:T(4,128)S(1)}, f32[4,2048]{1,0:T(4,128)S(1)}, u32[]{:S(2)}, u32[]{:S(2)}) collective-permute-start(f32[4,2048]{1,0:T(4,128)S(1)} %get-tuple-element.76), channel_id=1, source_target_pairs={{0,1},{1,0},{2,3},{3,2},{4,5},{5,4},{6,7},{7,6},{8,9},{9,8},{10,11... | collective-permute-start | bytes 98312 | tf_op jit(solution)/shard_map/ppermute | solution.py:25
  84.5 5.6 %collective-permute-start.9 = (f32[4,1024]{1,0:T(4,128)S(1)}, f32[4,1024]{1,0:T(4,128)S(1)}, u32[]{:S(2)}, u32[]{:S(2)}) collective-permute-start(f32[4,1024]{1,0:T(4,128)S(1)} %get-tuple-element.80), channel_id=1, source_target_pairs={{0,2},{1,3},{2,0},{3,1},{4,6},{5,7},{6,4},{7,5},{8,10},{9,11},{10,... | collective-permute-start | bytes 49160 | tf_op jit(solution)/shard_map/ppermute | solution.py:25
  90.2 9.7 %collective-permute-start.10 = (f32[4,512]{1,0:T(4,128)S(1)}, f32[4,512]{1,0:T(4,128)S(1)}, u32[]{:S(2)}, u32[]{:S(2)}) collective-permute-start(f32[4,512]{1,0:T(4,128)S(1)} %get-tuple-element.87), channel_id=1, source_target_pairs={{0,4},{1,5},{2,6},{3,7},{4,0},{5,1},{6,2},{7,3},{8,12},{9,13},{10,... | collective-permute-start | bytes 24584 | tf_op jit(solution)/shard_map/ppermute | solution.py:25
  99.9 9.8 %collective-permute-start.11 = (f32[4,256]{1,0:T(4,128)S(1)}, f32[4,256]{1,0:T(4,128)S(1)}, u32[]{:S(2)}, u32[]{:S(2)}) collective-permute-start(f32[4,256]{1,0:T(4,128)S(1)} %get-tuple-element.94), channel_id=1, source_target_pairs={{0,8},{1,9},{2,10},{3,11},{4,12},{5,13},{6,14},{7,15},{8,0},{9,1},... | collective-permute-start | bytes 12296 | tf_op jit(solution)/shard_map/ppermute | solution.py:25
  109.8 14.2 %collective-permute-start.12 = (f32[4,128]{1,0:T(4,128)S(1)}, f32[4,128]{1,0:T(4,128)S(1)}, u32[]{:S(2)}, u32[]{:S(2)}) collective-permute-start(f32[4,128]{1,0:T(4,128)S(1)} %get-tuple-element.101), channel_id=1, source_target_pairs={{0,16},{1,17},{2,18},{3,19},{4,20},{5,21},{6,22},{7,23},{8,24},{9,... | collective-permute-start | bytes 6152 | tf_op jit(solution)/shard_map/ppermute | solution.py:25
where the time goes:
time: 125 us
  starting transfers between devices  55.3 us (44%)
  waiting for transfers between devices  37.1 us (30%)
  local copies, waits for them, and re-layouts  13.7 us (11%)
  matrix products  11.9 us (10%)
  other arithmetic  5.84 us (5%)
    ppermute x5, starting transfers between devices, swapped(): lax.ppermute(array, axis, [(i, i ^ 1 << distance) for i in range(lax.axis...  33 us
    ppermute x4, waiting for transfers between devices, padded_2(): before = lax.ppermute(last, axis, up)  15.4 us
    ppermute x4, starting transfers between devices, padded_2(): after = lax.ppermute(initial, axis, down)  11.9 us
    dot_general x8, matrix products, one_layer(): jnp.einsum('tk,kyx->tyx', tables, hats, precision=lax.Precision.HIGHEST)  11.7 us
    ppermute x4, waiting for transfers between devices, padded_2(): after = lax.ppermute(initial, axis, down)  11 us
    dynamic_update_slice x16, local copies, waits for them, and re-layouts, table_lookup(): stacked = lax.map(one_layer, position)  11 us
    ppermute x5, waiting for transfers between devices, swapped(): lax.ppermute(array, axis, [(i, i ^ 1 << distance) for i in range(lax.axis...  10.6 us
    ppermute x4, starting transfers between devices, padded_2(): before = lax.ppermute(last, axis, up)  10.4 us
  transfers between devices with their start and end apart: 13, of which 11 were waited for; matrix products, arithmetic and copies ran while one was open for 19% of the time, Pallas kernels for 0%

commit v1 on v0

v1 whole, which is shorter than its diff:
```python
import functools

import jax
import jax.numpy as jnp
import ml_dtypes
import numpy as np
from jax import lax
from jax.experimental import pallas as pl
from jax.experimental.pallas import tpu as pltpu
from jax.sharding import PartitionSpec as P

TAPS = (0.0625, 0.25, 0.375, 0.25, 0.0625)
LIGHT = (0.64, 0.6, 0.48)
MESH = pl.DeviceIdType.MESH
F32 = jnp.float32
BF16 = jnp.bfloat16


def tap(distance):
    return TAPS[distance + 2] if -2 <= distance <= 2 else 0.0


def depth_height_weights(layers, height):
    along_z = np.array([[tap(z - (i - 2)) for z in range(layers)] for i in range(layers + 4)])
    along_y = np.array([[tap(yy - y) for yy in range(height)] for y in range(height)])
    return np.kron(along_z, along_y).astype(ml_dtypes.bfloat16)


def width_weights(width):
    result = np.zeros((3, 2, 2 * width, 2 * width))
    for kind in range(3):
        cells = np.arange(-3, width + 3)
        full = np.array([[tap(c - x) for x in range(-1, width + 1)] for c in cells])
        if kind == 0:
            full[:3] = 0.0
            full[:, 0] = 0.0
        if kind == 2:
            full[-3:] = 0.0
            full[:, -1] = 0.0
        both = np.concatenate([full[:, 1:-1], 0.5 * (full[:, 2:] - full[:, :-2])], axis=1)
        for slot in range(2):
            result[kind, slot, :width] = both[3:-3]
            result[kind, slot, width + 4 * slot : width + 4 * slot + 3] = both[:3]
            result[kind, slot, width + 8 + 4 * slot : width + 8 + 4 * slot + 3] = both[-3:]
    return result.astype(ml_dtypes.bfloat16)


def edge_selector(width):
    result = np.zeros((16, 2 * width))
    for slot in range(2):
        for c in range(3):
            result[4 * slot + c, slot * width + width - 3 + c] = 1.0
            result[8 + 4 * slot + c, slot * width + c] = 1.0
    return result.astype(ml_dtypes.bfloat16)


def halves(values):
    high = values.astype(BF16)
    return high, (values - high.astype(F32)).astype(BF16)


def dot(a, b, dims=((1,), (0,))):
    return lax.dot_general(a, b, (dims, ((), ())), preferred_element_type=F32)


def kernel(
    n_gx, n_depth, cells_z,
    vol_hbm, ext_hbm, pal_hbm, pidx_hbm, zy_hbm, xw_hbm, sel_hbm,
    out_ref,
    vol, ext, pal, pidx, zy, xw, sel, tab,
    part, edge_out, edge_in, corner_in, z01_in, z23_in,
    smooth, slope, piece_out, piece_in,
    load_sem, send_sem, recv_sem, piece_send, piece_recv,
):
    gx = lax.axis_index("gx")
    me = lax.axis_index("depth")
    left, right = lax.rem(gx + n_gx - 1, n_gx), lax.rem(gx + 1, n_gx)
    near, far = lax.rem(me + n_depth - 1, n_depth), lax.rem(me + 1, n_depth)
    layers, height, width = vol.shape[1], vol.shape[2], vol.shape[3]

    kind = jnp.where(gx == 0, 0, jnp.where(gx == n_gx - 1, 2, 1))
    loads = [
        pltpu.make_async_copy(vol_hbm, vol, load_sem.at[0]),
        pltpu.make_async_copy(zy_hbm, zy, load_sem.at[1]),
        pltpu.make_async_copy(sel_hbm, sel, load_sem.at[2]),
        pltpu.make_async_copy(xw_hbm.at[kind], xw, load_sem.at[3]),
        pltpu.make_async_copy(ext_hbm, ext, load_sem.at[4]),
        pltpu.make_async_copy(pal_hbm, pal, load_sem.at[5]),
        pltpu.make_async_copy(pidx_hbm, pidx, load_sem.at[6]),
    ]
    for load in loads:
        load.start()

    barrier = pltpu.get_barrier_semaphore()
    for gx_to in (left, right):
        for depth_to in (near, me, far):
            pl.semaphore_signal(barrier, inc=1, device_id=(gx_to, depth_to), device_id_type=MESH)

    @pl.loop(1, n_depth)
    def _(step):
        to = lax.rem(me + step, n_depth)
        pl.semaphore_signal(barrier, inc=1, device_id=(gx, to), device_id_type=MESH)

    for load in loads[:3]:
        load.wait()

    for pair in range(2):
        raw = jnp.concatenate(
            [vol[2 * pair + f].reshape(layers * height, width) for f in range(2)], axis=1
        )
        high, low = halves(raw)
        spread = dot(zy[...], high) + dot(zy[...], low)
        for f in range(2):
            part[2 * pair + f] = spread[:, f * width : (f + 1) * width].reshape(
                layers + 4, height, width
            )
        high, low = halves(spread)
        edges = dot(sel[...], high, ((1,), (1,))) + dot(sel[...], low, ((1,), (1,)))
        for side in range(2):
            for k in range(3):
                edge_out[side, k, pair] = edges[
                    8 * side : 8 * side + 8, 128 * k : 128 * k + 128
                ]

    pl.semaphore_wait(barrier, n_depth + 5)

    def send(number, source, target, gx_to, depth_to):
        copy = pltpu.make_async_remote_copy(
            src_ref=source,
            dst_ref=target,
            send_sem=send_sem.at[number],
            recv_sem=recv_sem.at[number],
            device_id=(gx_to, depth_to),
            device_id_type=MESH,
        )
        copy.start()
        return copy

    copies = [
        send(0, part.at[pl.ds(0, 2), pl.ds(layers + 1, 3)], z01_in.at[0], gx, far),
        send(1, part.at[pl.ds(0, 2), pl.ds(0, 3)], z01_in.at[1], gx, near),
        send(2, part.at[pl.ds(2, 2), pl.ds(layers + 2, 2)], z23_in.at[0], gx, far),
        send(3, part.at[pl.ds(2, 2), pl.ds(0, 2)], z23_in.at[1], gx, near),
        send(4, edge_out.at[0, 2], corner_in.at[0, 0], right, far),
        send(5, edge_out.at[1, 2], corner_in.at[0, 1], left, far),
        send(6, edge_out.at[0, 0], corner_in.at[1, 0], right, near),
        send(7, edge_out.at[1, 0], corner_in.at[1, 1], left, near),
        send(8, edge_out.at[0], edge_in.at[0], right, me),
        send(9, edge_out.at[1], edge_in.at[1], left, me),
    ]

    for load in loads[3:]:
        load.wait()

    step_len = 0.25 / cells_z
    rows = lax.broadcasted_iota(jnp.int32, (pal.shape[0], 128), 0)
    chosen = pidx[...] == rows
    entries = [ext[...] * step_len] + [
        jnp.sum(jnp.where(chosen, pal[:, c : c + 1], 0.0), axis=0, keepdims=True)
        for c in range(3)
    ]
    table = jnp.concatenate(entries, axis=0)
    tab[0:4] = table
    tab[4:8] = jnp.concatenate([table[:, 1:], table[:, :1]], axis=1) - table

    zeros8 = jnp.zeros((layers + 4, 8, width), F32)
    for f in range(2):
        smooth[f, :, 0:8] = zeros8
        smooth[f, :, height + 8 : height + 16] = zeros8

    for copy in copies:
        copy.wait_recv()

    has_near = jnp.where(me > 0, 1.0, 0.0).astype(F32)
    has_far = jnp.where(me < n_depth - 1, 1.0, 0.0).astype(F32)
    for k in range(3):
        for pair in range(2):
            edge = jnp.concatenate([edge_in[0, k, pair], edge_in[1, k, pair]], axis=0)
            if k == 0:
                edge += has_near * jnp.concatenate(
                    [corner_in[0, 0, pair], corner_in[0, 1, pair]], axis=0
                )
            if k == 2:
                edge += has_far * jnp.concatenate(
                    [corner_in[1, 0, pair], corner_in[1, 1, pair]], axis=0
                )
            edge = jnp.concatenate([edge, jnp.zeros((112, 128), F32)], axis=0)
            edge = jnp.transpose(edge)
            for f in range(2):
                field = 2 * pair + f
                body = [part[field, 4 * k + j] for j in range(4)]
                if pair == 0 and k == 0:
                    body = [body[0]] + [body[1 + j] + has_near * z01_in[0, f, j] for j in range(3)]
                if pair == 0 and k == 2:
                    body = [body[j] + has_far * z01_in[1, f, j] for j in range(3)] + [body[3]]
                if pair == 1 and k == 0:
                    body = body[:2] + [body[2 + j] + has_near * z23_in[0, f, j] for j in range(2)]
                if pair == 1 and k == 2:
                    body = [body[j] + has_far * z23_in[1, f, j] for j in range(2)] + body[2:]
                rows = jnp.concatenate(body, axis=0)
                high, low = halves(jnp.concatenate([rows, edge], axis=1))
                if pair == 0:
                    weights = xw[f]
                    found = dot(high, weights) + dot(low, weights)
                    here = found[:, :width].reshape(4, height, width)
                    for j in range(4):
                        layer = here[j]
                        if 4 * k + j == 1:
                            layer = layer * has_near
                        if 4 * k + j == layers + 2:
                            layer = layer * has_far
                        smooth[field, 4 * k + j, 8 : height + 8] = layer
                    slope[f, 4 * k : 4 * k + 4] = found[:, width:].reshape(4, height, width)
                else:
                    weights = xw[f, :, :width]
                    found = dot(high, weights) + dot(low, weights)
                    smooth[field, 4 * k : 4 * k + 4, 8 : height + 8] = found.reshape(
                        4, height, width
                    )

    top = ext.shape[1] - 1

    def look(row, at, fraction):
        def pick(r):
            entry = jnp.broadcast_to(tab[r : r + 1], (layers * 8, 128))
            return jnp.take_along_axis(entry, at, axis=1, mode="promise_in_bounds")

        return (pick(row) + fraction * pick(row + 4)).reshape(layers, 8, width)

    for t in range(height // 8):
        here = pl.ds(8 * t + 8, 8)
        grads = []
        for f in range(2):
            grads.append(
                (
                    0.5 * (smooth[f, 3 : layers + 3, here] - smooth[f, 1 : layers + 1, here]),
                    0.5
                    * (
                        smooth[f, 2 : layers + 2, 8 * t + 9 : 8 * t + 17]
                        - smooth[f, 2 : layers + 2, 8 * t + 7 : 8 * t + 15]
                    ),
                    slope[f, 2 : layers + 2, pl.ds(8 * t, 8)],
                )
            )
        z0, y0, x0 = grads[0]
        z1, y1, x1 = grads[1]
        facing = LIGHT[0] * z0 + LIGHT[1] * y0 + LIGHT[2] * x0
        steep = z0 * z0 + y0 * y0 + x0 * x0
        shading = 0.35 + 0.65 * facing * facing / (steep + 0.05)
        warm = z1 * z1 + y1 * y1 + x1 * x1
        gain = 0.25 + 1.5 * warm / (warm + 0.1)
        place = (0.5 * top) * (1.0 + jnp.tanh(smooth[0, 2 : layers + 2, here]))
        at = jnp.clip(place.astype(jnp.int32), 0, top - 1)
        fraction = (place - at.astype(F32)).reshape(layers * 8, width)
        at = at.reshape(layers * 8, width)
        tau = look(0, at, fraction) * gain
        bright = (
            (1.0 + 0.5 * jnp.tanh(smooth[2, 2 : layers + 2, here]))
            * jnp.exp(0.5 * jnp.tanh(smooth[3, 2 : layers + 2, here]))
            * shading
        )
        absorbed = tau * (
            1.0
            - tau * (1 / 2)
            * (1.0 - tau * (1 / 3) * (1.0 - tau * (1 / 4) * (1.0 - tau * (1 / 5) * (1.0 - tau * (1 / 6)))))
        )
        opaque = jnp.zeros((8, width), F32)
        weights = []
        for z in range(layers):
            weight = absorbed[z] - absorbed[z] * opaque
            weights.append(weight[None])
            opaque = opaque + weight
        weight = jnp.concatenate(weights, axis=0) * bright
        for c in range(3):
            piece_out[pl.ds(8 * t, 8), c] = jnp.sum(weight * look(1 + c, at, fraction), axis=0)
        piece_out[pl.ds(8 * t, 8), 3] = opaque

    def piece(to):
        return pltpu.make_async_remote_copy(
            src_ref=piece_out.at[to],
            dst_ref=piece_in.at[me],
            send_sem=piece_send,
            recv_sem=piece_recv,
            device_id=(gx, to),
            device_id_type=MESH,
        )

    @pl.loop(1, n_depth)
    def _(step):
        piece(lax.rem(me + step, n_depth)).start()

    own = pltpu.make_async_copy(piece_out.at[me], piece_in.at[me], piece_recv)
    own.start()
    for copy in copies:
        copy.wait_send()
    pltpu.make_async_copy(piece_in, piece_in, piece_recv).wait()
    others = piece_out.at[pl.ds(0, n_depth - 1)]
    pltpu.make_async_copy(others, others, piece_send).wait()

    group = n_depth // 8

    def over(nearer, farther):
        through = 1.0 - nearer[3]
        return [nearer[c] + through * farther[c] for c in range(4)]

    pieces = [
        [jnp.concatenate([piece_in[s * group + j, c : c + 1] for s in range(8)], axis=0) for c in range(4)]
        for j in range(group)
    ]
    total = pieces[0]
    for j in range(1, group):
        total = over(total, pieces[j])
    size = 8
    while size > 1:
        size //= 2
        nearer = [jnp.concatenate([v[2 * i : 2 * i + 1] for i in range(size)], axis=0) for v in total]
        farther = [jnp.concatenate([v[2 * i + 1 : 2 * i + 2] for i in range(size)], axis=0) for v in total]
        total = over(nearer, farther)
    out_ref[...] = jnp.concatenate(total, axis=0)


def solution(mesh):
    n_gx, n_depth = mesh.shape["gx"], mesh.shape["depth"]

    def per_device(volume, extinction, palette, palette_index):
        fields, layers, height, width = volume.shape
        entries = extinction.shape[0]
        colours = palette.shape[0]
        zy = depth_height_weights(layers, height)
        xw = width_weights(width)
        sel = edge_selector(width)
        anywhere = pl.BlockSpec(memory_space=pl.ANY)
        image = pl.pallas_call(
            functools.partial(kernel, n_gx, n_depth, layers * n_depth),
            out_shape=jax.ShapeDtypeStruct((4, width), F32),
            in_specs=[anywhere] * 7,
            out_specs=pl.BlockSpec(memory_space=pltpu.VMEM),
            scratch_shapes=[
                pltpu.VMEM(volume.shape, F32),
                pltpu.VMEM((1, entries), F32),
                pltpu.VMEM((colours, 3), F32),
                pltpu.VMEM((1, entries), jnp.int32),
                pltpu.VMEM(zy.shape, BF16),
                pltpu.VMEM(xw.shape[1:], BF16),
                pltpu.VMEM(sel.shape, BF16),
                pltpu.VMEM((8, entries), F32),
                pltpu.VMEM((fields, layers + 4, height, width), F32),
                pltpu.VMEM((2, 3, 2, 8, 128), F32),
                pltpu.VMEM((2, 3, 2, 8, 128), F32),
                pltpu.VMEM((2, 2, 2, 8, 128), F32),
                pltpu.VMEM((2, 2, 3, height, width), F32),
                pltpu.VMEM((2, 2, 2, height, width), F32),
                pltpu.VMEM((fields, layers + 4, height + 16, width), F32),
                pltpu.VMEM((2, layers + 4, height, width), F32),
                pltpu.VMEM((n_depth, 4, width), F32),
                pltpu.VMEM((n_depth, 4, width), F32),
                pltpu.SemaphoreType.DMA((7,)),
                pltpu.SemaphoreType.DMA((10,)),
                pltpu.SemaphoreType.DMA((10,)),
                pltpu.SemaphoreType.DMA,
                pltpu.SemaphoreType.DMA,
            ],
            compiler_params=pltpu.CompilerParams(
                collective_id=0, has_side_effects=True, vmem_limit_bytes=32 * 1024 * 1024
            ),
        )(
            volume,
            extinction.reshape(1, entries),
            palette,
            palette_index.reshape(1, entries),
            jnp.asarray(zy),
            jnp.asarray(xw),
            jnp.asarray(sel),
        )
        return image.reshape(4, 1, width)

    placed = (P(None, "depth", None, "gx"), P(), P(), P())
    return jax.shard_map(
        per_device, mesh=mesh, in_specs=placed, out_specs=P(None, "gx", "depth"), check_vma=False
    )
```

time: 125 us -> 38 us (0.30)
  the two profiles are of different devices: /device:TPU:38 before, /device:TPU:1 now
where the time goes in v1:
time: 38 us; the launch traced here: 37.7 us
  Pallas kernels  33.2 us (87%)
  local copies, waits for them, and re-layouts  4.48 us (12%)
    pallas_call x1, Pallas kernels, per_device(): pl.pallas_call(functools.partial(kernel, n_gx, n_depth, layers * n_depth)...  33.2 us
    unnamed x14, local copies, waits for them, and re-layouts  4.48 us

profile of v1, /device:TPU:1, one launch (start us, length us, event | category | flops | bytes accessed | tf_op | source)
XLA Modules:
  0.0 37.7 jit_solution(17360167238982953548)
XLA Ops:
  0.0 0.0 copy-start.3
  0.0 0.0 copy-start.4
  0.0 0.0 copy-start.5
  0.0 0.8 %copy.8.pal_hbm = f32[16,3]{1,0:T(8,128)S(1)} copy(f32[16,3]{0,1:T(4,128)} %param.9) | data formatting | bytes 384 | tf_op args[2]
  0.8 0.0 copy-done.3
  0.8 0.0 copy-done.4
  0.8 0.0 copy-done.5
  0.8 0.0 copy-start
  0.8 1.1 %copy-done = bf16[3,2,256,256]{3,2,1,0:T(8,128)(2,1)S(1)} copy-done((bf16[3,2,256,256]{3,2,1,0:T(8,128)(2,1)S(1)}, bf16[3,2,256,256]{3,2,1,0:T(8,128)(2,1)}, u32[]{:S(2)}) %copy-start) | copy-done | bytes 786456
  2.0 0.0 copy-start.1
  2.0 1.0 %copy-done.1 = f32[4,8,32,128]{3,2,1,0:T(8,128)S(1)} copy-done((f32[4,8,32,128]{3,2,1,0:T(8,128)S(1)}, f32[4,8,32,128]{3,2,1,0:T(8,128)}, u32[]{:S(2)}) %copy-start.1) | copy-done | bytes 524312
  3.0 0.0 copy-start.2
  3.0 0.9 %copy-done.2 = bf16[384,256]{1,0:T(8,128)(2,1)S(1)} copy-done((bf16[384,256]{1,0:T(8,128)(2,1)S(1)}, bf16[384,256]{1,0:T(8,128)(2,1)}, u32[]{:S(2)}) %copy-start.2) | copy-done | bytes 196632
  3.9 33.2 %shard_map.73 = f32[4,128]{1,0:T(4,128)S(1)} custom-call(f32[4,8,32,128]{3,2,1,0:T(8,128)S(1)} %copy-done.1, f32[1,128]{1,0:T(1,128)S(1)} %bitcast.6, f32[16,3]{1,0:T(8,128)S(1)} %copy.8.pal_hbm, s32[1,128]{1,0:T(1,128)S(1)} %bitcast.7, bf16[384,256]{1,0:T(8,128)(2,1)S(1)} %copy-done.2, bf16[3,2,256,256]{3,2,1,0:T(8,128)(2,1)S(1)} %copy-done, ...), custom_call_target="tpu_custom_call" | custom-call | tf_op jit(solution)/shard_map/pallas_call | solution.py:333
  37.1 0.6 %copy.11 = f32[4,1,128]{2,1,0:T(1,128)} copy(f32[4,1,128]{2,1,0:T(1,128)S(1)} %bitcast.5) | data formatting | bytes 4096
Async XLA Ops:
  0.0 0.8 %copy-start.3 = (bf16[16,256]{1,0:T(8,128)(2,1)S(1)}, bf16[16,256]{1,0:T(8,128)(2,1)}, u32[]{:S(2)}) copy-start(bf16[16,256]{1,0:T(8,128)(2,1)} %constant.8.clone.sel_hbm) | copy-start | bytes 24580
  0.0 0.8 %copy-start.4 = (f32[128]{0:T(128)S(1)}, f32[128]{0:T(128)}, u32[]{:S(2)}) copy-start(f32[128]{0:T(128)} %param.8) | copy-start | bytes 1540
  0.0 0.8 %copy-start.5 = (s32[128]{0:T(128)S(1)}, s32[128]{0:T(128)}, u32[]{:S(2)}) copy-start(s32[128]{0:T(128)} %param.10) | copy-start | bytes 1540
  0.8 1.1 %copy-start = (bf16[3,2,256,256]{3,2,1,0:T(8,128)(2,1)S(1)}, bf16[3,2,256,256]{3,2,1,0:T(8,128)(2,1)}, u32[]{:S(2)}) copy-start(bf16[3,2,256,256]{3,2,1,0:T(8,128)(2,1)} %constant.7.clone.xw_hbm) | copy-start | bytes 2359300
  2.0 1.0 %copy-start.1 = (f32[4,8,32,128]{3,2,1,0:T(8,128)S(1)}, f32[4,8,32,128]{3,2,1,0:T(8,128)}, u32[]{:S(2)}) copy-start(f32[4,8,32,128]{3,2,1,0:T(8,128)} %vol_hbm.1) | copy-start | bytes 1572868
  3.0 0.9 %copy-start.2 = (bf16[384,256]{1,0:T(8,128)(2,1)S(1)}, bf16[384,256]{1,0:T(8,128)(2,1)}, u32[]{:S(2)}) copy-start(bf16[384,256]{1,0:T(8,128)(2,1)} %constant.6.clone.zy_hbm) | copy-start | bytes 589828

commit v2 on v1

--- a/solution.py
+++ b/solution.py
@@ -12,6 +12,8 @@
 TAPS = (0.0625, 0.25, 0.375, 0.25, 0.0625)
 LIGHT = (0.64, 0.6, 0.48)
 MESH = pl.DeviceIdType.MESH
+SEND_ORDER = (4, 5, 6, 7, 8, 9, 0, 1, 2, 3)
+VMEM_BYTES = 63 * 1024 * 1024
 F32 = jnp.float32
 BF16 = jnp.bfloat16
 
@@ -70,17 +72,37 @@
     vol, ext, pal, pidx, zy, xw, sel, tab,
     part, edge_out, edge_in, corner_in, z01_in, z23_in,
     smooth, slope, piece_out, piece_in,
-    load_sem, send_sem, recv_sem, piece_send, piece_recv,
+    load_sem, send_sem, recv_sem, piece_send, piece_recv, known_sem,
 ):
     gx = lax.axis_index("gx")
     me = lax.axis_index("depth")
-    left, right = lax.rem(gx + n_gx - 1, n_gx), lax.rem(gx + 1, n_gx)
-    near, far = lax.rem(me + n_depth - 1, n_depth), lax.rem(me + 1, n_depth)
     layers, height, width = vol.shape[1], vol.shape[2], vol.shape[3]
-
-    kind = jnp.where(gx == 0, 0, jnp.where(gx == n_gx - 1, 2, 1))
+    has_left, has_right = gx > 0, gx < n_gx - 1
+    has_near, has_far = me > 0, me < n_depth - 1
+
+    first = pltpu.make_async_copy(vol_hbm, vol, load_sem.at[0])
+    first.start()
+
+    barrier = pltpu.get_barrier_semaphore()
+
+    def around(distance):
+        return lax.rem(me + n_depth + distance, n_depth)
+
+    def greet(gx_to, depth_to, there):
+        @pl.when(there)
+        def _():
+            pl.semaphore_signal(barrier, inc=1, device_id=(gx_to, depth_to), device_id_type=MESH)
+
+    for step, there in ((-1, has_near), (1, has_far), (0, True)):
+        greet(gx - 1, me + step, has_left & there)
+        greet(gx + 1, me + step, has_right & there)
+    reach = 4
+    for distance in range(1, reach + 1):
+        for depth_to in (around(distance), around(-distance)):
+            pl.semaphore_signal(barrier, inc=1, device_id=(gx, depth_to), device_id_type=MESH)
+
+    kind = jnp.where(has_left, jnp.where(has_right, 1, 2), 0)
     loads = [
-        pltpu.make_async_copy(vol_hbm, vol, load_sem.at[0]),
         pltpu.make_async_copy(zy_hbm, zy, load_sem.at[1]),
         pltpu.make_async_copy(sel_hbm, sel, load_sem.at[2]),
         pltpu.make_async_copy(xw_hbm.at[kind], xw, load_sem.at[3]),
@@ -90,17 +112,7 @@
     ]
     for load in loads:
         load.start()
-
-    barrier = pltpu.get_barrier_semaphore()
-    for gx_to in (left, right):
-        for depth_to in (near, me, far):
-            pl.semaphore_signal(barrier, inc=1, device_id=(gx_to, depth_to), device_id_type=MESH)
-
-    @pl.loop(1, n_depth)
-    def _(step):
-        to = lax.rem(me + step, n_depth)
-        pl.semaphore_signal(barrier, inc=1, device_id=(gx, to), device_id_type=MESH)
-
+    loads = [first] + loads
     for load in loads[:3]:
         load.wait()
 
@@ -122,10 +134,27 @@
                     8 * side : 8 * side + 8, 128 * k : 128 * k + 128
                 ]
 
-    pl.semaphore_wait(barrier, n_depth + 5)
-
-    def send(number, source, target, gx_to, depth_to):
-        copy = pltpu.make_async_remote_copy(
+    n_sides = has_left.astype(jnp.int32) + has_right.astype(jnp.int32)
+    n_rows = 1 + has_near.astype(jnp.int32) + has_far.astype(jnp.int32)
+    pl.semaphore_wait(barrier, 2 * reach + n_sides * n_rows)
+
+    near2, far2 = pl.ds(0, 2), pl.ds(2, 2)
+    table = [
+        (part.at[near2, pl.ds(layers + 1, 3)], z01_in.at[0], gx, me + 1, has_far, has_near),
+        (part.at[near2, pl.ds(0, 3)], z01_in.at[1], gx, me - 1, has_near, has_far),
+        (part.at[far2, pl.ds(layers + 2, 2)], z23_in.at[0], gx, me + 1, has_far, has_near),
+        (part.at[far2, pl.ds(0, 2)], z23_in.at[1], gx, me - 1, has_near, has_far),
+        (edge_out.at[0, 2], corner_in.at[0, 0], gx + 1, me + 1, has_right & has_far, has_left & has_near),
+        (edge_out.at[1, 2], corner_in.at[0, 1], gx - 1, me + 1, has_left & has_far, has_right & has_near),
+        (edge_out.at[0, 0], corner_in.at[1, 0], gx + 1, me - 1, has_right & has_near, has_left & has_far),
+        (edge_out.at[1, 0], corner_in.at[1, 1], gx - 1, me - 1, has_left & has_near, has_right & has_far),
+        (edge_out.at[0], edge_in.at[0], gx + 1, me, has_right, has_left),
+        (edge_out.at[1], edge_in.at[1], gx - 1, me, has_left, has_right),
+    ]
+
+    def copy(number):
+        source, target, gx_to, depth_to = table[number][:4]
+        return pltpu.make_async_remote_copy(
             src_ref=source,
             dst_ref=target,
             send_sem=send_sem.at[number],
@@ -133,90 +162,107 @@
             device_id=(gx_to, depth_to),
             device_id_type=MESH,
         )
-        copy.start()
-        return copy
-
-    copies = [
-        send(0, part.at[pl.ds(0, 2), pl.ds(layers + 1, 3)], z01_in.at[0], gx, far),
-        send(1, part.at[pl.ds(0, 2), pl.ds(0, 3)], z01_in.at[1], gx, near),
-        send(2, part.at[pl.ds(2, 2), pl.ds(layers + 2, 2)], z23_in.at[0], gx, far),
-        send(3, part.at[pl.ds(2, 2), pl.ds(0, 2)], z23_in.at[1], gx, near),
-        send(4, edge_out.at[0, 2], corner_in.at[0, 0], right, far),
-        send(5, edge_out.at[1, 2], corner_in.at[0, 1], left, far),
-        send(6, edge_out.at[0, 0], corner_in.at[1, 0], right, near),
-        send(7, edge_out.at[1, 0], corner_in.at[1, 1], left, near),
-        send(8, edge_out.at[0], edge_in.at[0], right, me),
-        send(9, edge_out.at[1], edge_in.at[1], left, me),
-    ]
+
+    for number in SEND_ORDER:
+        @pl.when(table[number][4])
+        def _():
+            copy(number).start()
+
+    def know():
+        for depth_to in (around(reach), around(-reach)):
+            pl.semaphore_signal(
+                known_sem.at[reach.bit_length() - 3], inc=1, device_id=(gx, depth_to), device_id_type=MESH
+            )
+
+    know()
+    for _, target, _, _, _, comes in table:
+        @pl.when(jnp.logical_not(comes))
+        def _():
+            target[...] = jnp.zeros(target.shape, F32)
 
     for load in loads[3:]:
         load.wait()
 
     step_len = 0.25 / cells_z
-    rows = lax.broadcasted_iota(jnp.int32, (pal.shape[0], 128), 0)
-    chosen = pidx[...] == rows
+    colours = pal.shape[1]
+    spread = jnp.concatenate([pal[...], jnp.zeros((3, 128 - colours), F32)], axis=1)
+    chosen = jnp.broadcast_to(pidx[...], (8, 128))
     entries = [ext[...] * step_len] + [
-        jnp.sum(jnp.where(chosen, pal[:, c : c + 1], 0.0), axis=0, keepdims=True)
+        jnp.take_along_axis(
+            jnp.broadcast_to(spread[c : c + 1], (8, 128)), chosen, axis=1, mode="promise_in_bounds"
+        )[0:1]
         for c in range(3)
     ]
-    table = jnp.concatenate(entries, axis=0)
-    tab[0:4] = table
-    tab[4:8] = jnp.concatenate([table[:, 1:], table[:, :1]], axis=1) - table
+    entries = jnp.concatenate(entries, axis=0)
+    tab[0:4] = entries
+    tab[4:8] = jnp.concatenate([entries[:, 1:], entries[:, :1]], axis=1) - entries
 
     zeros8 = jnp.zeros((layers + 4, 8, width), F32)
     for f in range(2):
         smooth[f, :, 0:8] = zeros8
         smooth[f, :, height + 8 : height + 16] = zeros8
 
-    for copy in copies:
-        copy.wait_recv()
-
-    has_near = jnp.where(me > 0, 1.0, 0.0).astype(F32)
-    has_far = jnp.where(me < n_depth - 1, 1.0, 0.0).astype(F32)
-    for k in range(3):
-        for pair in range(2):
-            edge = jnp.concatenate([edge_in[0, k, pair], edge_in[1, k, pair]], axis=0)
+    while 2 * reach < n_depth // 2:
+        pl.semaphore_wait(known_sem.at[reach.bit_length() - 3], 2)
+        reach *= 2
+        know()
+
+    def arrived(*numbers):
+        for number in numbers:
+            @pl.when(table[number][5])
+            def _():
+                copy(number).wait_recv()
+
+    keep_near = jnp.where(has_near, 1.0, 0.0).astype(F32)
+    keep_far = jnp.where(has_far, 1.0, 0.0).astype(F32)
+
+    def filter_width(k, pair):
+        edge = jnp.concatenate([edge_in[0, k, pair], edge_in[1, k, pair]], axis=0)
+        if k != 1:
+            edge += jnp.concatenate(
+                [corner_in[k // 2, 0, pair], corner_in[k // 2, 1, pair]], axis=0
+            )
+        edge = jnp.transpose(jnp.concatenate([edge, jnp.zeros((112, 128), F32)], axis=0))
+        for f in range(2):
+            field = 2 * pair + f
+            body = [part[field, 4 * k + j] for j in range(4)]
+            came, count = (z01_in, 3) if pair == 0 else (z23_in, 2)
             if k == 0:
-                edge += has_near * jnp.concatenate(
-                    [corner_in[0, 0, pair], corner_in[0, 1, pair]], axis=0
+                for j in range(count):
+                    body[4 - count + j] += came[0, f, j]
+            if k == 2:
+                for j in range(count):
+                    body[j] += came[1, f, j]
+            rows = jnp.concatenate(body, axis=0)
+            high, low = halves(jnp.concatenate([rows, edge], axis=1))
+            if pair == 0:
+                weights = xw[f]
+                found = dot(high, weights) + dot(low, weights)
+                here = found[:, :width].reshape(4, height, width)
+                for j in range(4):
+                    layer = here[j]
+                    if 4 * k + j == 1:
+                        layer = layer * keep_near
+                    if 4 * k + j == layers + 2:
+                        layer = layer * keep_far
+                    smooth[field, 4 * k + j, 8 : height + 8] = layer
+                slope[f, 4 * k : 4 * k + 4] = found[:, width:].reshape(4, height, width)
+            else:
+                weights = xw[f, :, :width]
+                found = dot(high, weights) + dot(low, weights)
+                smooth[field, 4 * k : 4 * k + 4, 8 : height + 8] = found.reshape(
+                    4, height, width
                 )
-            if k == 2:
-                edge += has_far * jnp.concatenate(
-                    [corner_in[1, 0, pair], corner_in[1, 1, pair]], axis=0
-                )
-            edge = jnp.concatenate([edge, jnp.zeros((112, 128), F32)], axis=0)
-            edge = jnp.transpose(edge)
-            for f in range(2):
-                field = 2 * pair + f
-                body = [part[field, 4 * k + j] for j in range(4)]
-                if pair == 0 and k == 0:
-                    body = [body[0]] + [body[1 + j] + has_near * z01_in[0, f, j] for j in range(3)]
-                if pair == 0 and k == 2:
-                    body = [body[j] + has_far * z01_in[1, f, j] for j in range(3)] + [body[3]]
-                if pair == 1 and k == 0:
-                    body = body[:2] + [body[2 + j] + has_near * z23_in[0, f, j] for j in range(2)]
-                if pair == 1 and k == 2:
-                    body = [body[j] + has_far * z23_in[1, f, j] for j in range(2)] + body[2:]
-                rows = jnp.concatenate(body, axis=0)
-                high, low = halves(jnp.concatenate([rows, edge], axis=1))
-                if pair == 0:
-                    weights = xw[f]
-                    found = dot(high, weights) + dot(low, weights)
-                    here = found[:, :width].reshape(4, height, width)
-                    for j in range(4):
-                        layer = here[j]
-                        if 4 * k + j == 1:
-                            layer = layer * has_near
-                        if 4 * k + j == layers + 2:
-                            layer = layer * has_far
-                        smooth[field, 4 * k + j, 8 : height + 8] = layer
-                    slope[f, 4 * k : 4 * k + 4] = found[:, width:].reshape(4, height, width)
-                else:
-                    weights = xw[f, :, :width]
-                    found = dot(high, weights) + dot(low, weights)
-                    smooth[field, 4 * k : 4 * k + 4, 8 : height + 8] = found.reshape(
-                        4, height, width
-                    )
+
+    arrived(8, 9)
+    filter_width(1, 0)
+    filter_width(1, 1)
+    arrived(4, 5, 6, 7, 0, 1)
+    filter_width(0, 0)
+    filter_width(2, 0)
+    arrived(2, 3)
+    filter_width(0, 1)
+    filter_width(2, 1)
 
     top = ext.shape[1] - 1
 
@@ -226,6 +272,16 @@
             return jnp.take_along_axis(entry, at, axis=1, mode="promise_in_bounds")
 
         return (pick(row) + fraction * pick(row + 4)).reshape(layers, 8, width)
+
+    def piece(to):
+        return pltpu.make_async_remote_copy(
+            src_ref=piece_out.at[to],
+            dst_ref=piece_in.at[me],
+            send_sem=piece_send,
+            recv_sem=piece_recv,
+            device_id=(gx, to),
+            device_id_type=MESH,
+        )
 
     for t in range(height // 8):
         here = pl.ds(8 * t + 8, 8)
@@ -274,25 +330,21 @@
         for c in range(3):
             piece_out[pl.ds(8 * t, 8), c] = jnp.sum(weight * look(1 + c, at, fraction), axis=0)
         piece_out[pl.ds(8 * t, 8), 3] = opaque
-
-    def piece(to):
-        return pltpu.make_async_remote_copy(
-            src_ref=piece_out.at[to],
-            dst_ref=piece_in.at[me],
-            send_sem=piece_send,
-            recv_sem=piece_recv,
-            device_id=(gx, to),
-            device_id_type=MESH,
-        )
-
-    @pl.loop(1, n_depth)
-    def _(step):
-        piece(lax.rem(me + step, n_depth)).start()
+        if t == 0:
+            pl.semaphore_wait(known_sem.at[reach.bit_length() - 3], 2)
+
+        @pl.loop(8 * t, 8 * t + 8)
+        def _(to):
+            @pl.when(to != me)
+            def _():
+                piece(to).start()
 
     own = pltpu.make_async_copy(piece_out.at[me], piece_in.at[me], piece_recv)
     own.start()
-    for copy in copies:
-        copy.wait_send()
+    for number in range(len(table)):
+        @pl.when(table[number][4])
+        def _():
+            copy(number).wait_send()
     pltpu.make_async_copy(piece_in, piece_in, piece_recv).wait()
     others = piece_out.at[pl.ds(0, n_depth - 1)]
     pltpu.make_async_copy(others, others, piece_send).wait()
@@ -338,7 +390,7 @@
             scratch_shapes=[
                 pltpu.VMEM(volume.shape, F32),
                 pltpu.VMEM((1, entries), F32),
-                pltpu.VMEM((colours, 3), F32),
+                pltpu.VMEM((3, colours), F32),
                 pltpu.VMEM((1, entries), jnp.int32),
                 pltpu.VMEM(zy.shape, BF16),
                 pltpu.VMEM(xw.shape[1:], BF16),
@@ -359,14 +411,15 @@
                 pltpu.SemaphoreType.DMA((10,)),
                 pltpu.SemaphoreType.DMA,
                 pltpu.SemaphoreType.DMA,
+                pltpu.SemaphoreType.REGULAR((2,)),
             ],
             compiler_params=pltpu.CompilerParams(
-                collective_id=0, has_side_effects=True, vmem_limit_bytes=32 * 1024 * 1024
+                collective_id=0, has_side_effects=True, vmem_limit_bytes=VMEM_BYTES
             ),
         )(
             volume,
             extinction.reshape(1, entries),
-            palette,
+            palette.T,
             palette_index.reshape(1, entries),
             jnp.asarray(zy),
             jnp.asarray(xw),

time: 38 us -> 27.6 us (0.73)
  the two profiles are of different devices: /device:TPU:1 before, /device:TPU:25 now
where the time goes in v2:
time: 27.6 us; the launch traced here: 27.4 us
  Pallas kernels  26.2 us (95%)
  local copies, waits for them, and re-layouts  1.26 us (5%)
    pallas_call x1, Pallas kernels, per_device(): pl.pallas_call(functools.partial(kernel, n_gx, n_depth, layers * n_depth)...  26.2 us
    unnamed x1, local copies, waits for them, and re-layouts  1.26 us

profile of v2, /device:TPU:25, one launch (start us, length us, event | category | flops | bytes accessed | tf_op | source)
XLA Modules:
  0.0 27.4 jit_solution(12002311868296726913)
XLA Ops:
  0.0 26.2 %shard_map.73 = f32[4,128]{1,0:T(4,128)} custom-call(f32[4,8,32,128]{3,2,1,0:T(8,128)} %vol_hbm.1, f32[1,128]{1,0:T(1,128)} %bitcast.8, f32[3,16]{1,0:T(4,128)} %bitcast.7, s32[1,128]{1,0:T(1,128)} %bitcast.9, bf16[384,256]{1,0:T(8,128)(2,1)} %constant.6.clone.zy_hbm, bf16[3,2,256,256]{3,2,1,0:T(8,128)(2,1)} %constant.7.clone.xw_hbm, ...), custom_call_target="tpu_custom_call" | custom-call | tf_op jit(solution)/shard_map/pallas_call | solution.py:385
  26.2 1.3 %copy.10 = f32[4,1,128]{2,1,0:T(1,128)} copy(f32[4,1,128]{2,1,0:T(1,128)} %bitcast.6) | data formatting | bytes 4096

commit v3 on v2

--- a/solution.py
+++ b/solution.py
@@ -12,7 +12,7 @@
 TAPS = (0.0625, 0.25, 0.375, 0.25, 0.0625)
 LIGHT = (0.64, 0.6, 0.48)
 MESH = pl.DeviceIdType.MESH
-SEND_ORDER = (4, 5, 6, 7, 8, 9, 0, 1, 2, 3)
+FIRST = 8
 VMEM_BYTES = 63 * 1024 * 1024
 F32 = jnp.float32
 BF16 = jnp.bfloat16
@@ -71,7 +71,7 @@
     out_ref,
     vol, ext, pal, pidx, zy, xw, sel, tab,
     part, edge_out, edge_in, corner_in, z01_in, z23_in,
-    smooth, slope, piece_out, piece_in,
+    beside, smooth, slope, piece_out, piece_in,
     load_sem, send_sem, recv_sem, piece_send, piece_recv, known_sem,
 ):
     gx = lax.axis_index("gx")
@@ -80,8 +80,19 @@
     has_left, has_right = gx > 0, gx < n_gx - 1
     has_near, has_far = me > 0, me < n_depth - 1
 
-    first = pltpu.make_async_copy(vol_hbm, vol, load_sem.at[0])
-    first.start()
+    kind = jnp.where(has_left, jnp.where(has_right, 1, 2), 0)
+    loads = [
+        pltpu.make_async_copy(vol_hbm.at[pl.ds(0, 2)], vol.at[pl.ds(0, 2)], load_sem.at[0]),
+        pltpu.make_async_copy(zy_hbm, zy, load_sem.at[1]),
+        pltpu.make_async_copy(vol_hbm.at[pl.ds(2, 2)], vol.at[pl.ds(2, 2)], load_sem.at[2]),
+        pltpu.make_async_copy(sel_hbm, sel, load_sem.at[3]),
+        pltpu.make_async_copy(xw_hbm.at[kind], xw, load_sem.at[4]),
+        pltpu.make_async_copy(ext_hbm, ext, load_sem.at[5]),
+        pltpu.make_async_copy(pal_hbm, pal, load_sem.at[6]),
+        pltpu.make_async_copy(pidx_hbm, pidx, load_sem.at[7]),
+    ]
+    for load in loads[:2]:
+        load.start()
 
     barrier = pltpu.get_barrier_semaphore()
 
@@ -97,26 +108,32 @@
         greet(gx - 1, me + step, has_left & there)
         greet(gx + 1, me + step, has_right & there)
     reach = 4
-    for distance in range(1, reach + 1):
+    for distance in range(reach, 0, -1):
         for depth_to in (around(distance), around(-distance)):
             pl.semaphore_signal(barrier, inc=1, device_id=(gx, depth_to), device_id_type=MESH)
-
-    kind = jnp.where(has_left, jnp.where(has_right, 1, 2), 0)
-    loads = [
-        pltpu.make_async_copy(zy_hbm, zy, load_sem.at[1]),
-        pltpu.make_async_copy(sel_hbm, sel, load_sem.at[2]),
-        pltpu.make_async_copy(xw_hbm.at[kind], xw, load_sem.at[3]),
-        pltpu.make_async_copy(ext_hbm, ext, load_sem.at[4]),
-        pltpu.make_async_copy(pal_hbm, pal, load_sem.at[5]),
-        pltpu.make_async_copy(pidx_hbm, pidx, load_sem.at[6]),
-    ]
-    for load in loads:
+    for load in loads[2:]:
         load.start()
-    loads = [first] + loads
-    for load in loads[:3]:
-        load.wait()
-
-    for pair in range(2):
+
+    @pl.when(me < FIRST)
+    def _():
+        @pl.loop(reach + 1, n_depth - reach)
+        def _(distance):
+            pl.semaphore_signal(
+                barrier, inc=1, device_id=(gx, around(distance)), device_id_type=MESH
+            )
+
+    n_first = 0
+    for device in range(FIRST):
+        apart = lax.rem(me + n_depth - device, n_depth)
+        n_first += ((apart > reach) & (apart < n_depth - reach)).astype(jnp.int32)
+
+    def know():
+        for depth_to in (around(reach), around(-reach)):
+            pl.semaphore_signal(
+                known_sem.at[reach.bit_length() - 3], inc=1, device_id=(gx, depth_to), device_id_type=MESH
+            )
+
+    def filter_own(pair):
         raw = jnp.concatenate(
             [vol[2 * pair + f].reshape(layers * height, width) for f in range(2)], axis=1
         )
@@ -134,16 +151,17 @@
                     8 * side : 8 * side + 8, 128 * k : 128 * k + 128
                 ]
 
+    for load in (loads[0], loads[1], loads[3]):
+        load.wait()
+    filter_own(0)
+    loads[2].wait()
+    filter_own(1)
     n_sides = has_left.astype(jnp.int32) + has_right.astype(jnp.int32)
     n_rows = 1 + has_near.astype(jnp.int32) + has_far.astype(jnp.int32)
-    pl.semaphore_wait(barrier, 2 * reach + n_sides * n_rows)
-
-    near2, far2 = pl.ds(0, 2), pl.ds(2, 2)
+    pl.semaphore_wait(barrier, 2 * reach + n_sides * n_rows + n_first)
+    know()
+
     table = [
-        (part.at[near2, pl.ds(layers + 1, 3)], z01_in.at[0], gx, me + 1, has_far, has_near),
-        (part.at[near2, pl.ds(0, 3)], z01_in.at[1], gx, me - 1, has_near, has_far),
-        (part.at[far2, pl.ds(layers + 2, 2)], z23_in.at[0], gx, me + 1, has_far, has_near),
-        (part.at[far2, pl.ds(0, 2)], z23_in.at[1], gx, me - 1, has_near, has_far),
         (edge_out.at[0, 2], corner_in.at[0, 0], gx + 1, me + 1, has_right & has_far, has_left & has_near),
         (edge_out.at[1, 2], corner_in.at[0, 1], gx - 1, me + 1, has_left & has_far, has_right & has_near),
         (edge_out.at[0, 0], corner_in.at[1, 0], gx + 1, me - 1, has_right & has_near, has_left & has_far),
@@ -151,6 +169,17 @@
         (edge_out.at[0], edge_in.at[0], gx + 1, me, has_right, has_left),
         (edge_out.at[1], edge_in.at[1], gx - 1, me, has_left, has_right),
     ]
+    half = height // 2
+    for h in range(2):
+        rows = pl.ds(h * half, half)
+        for fields, count, target in ((pl.ds(0, 2), 3, z01_in), (pl.ds(2, 2), 2, z23_in)):
+            last = pl.ds(layers + 4 - count, count)
+            table.append(
+                (part.at[fields, last, rows], target.at[0, h], gx, me + 1, has_far, has_near)
+            )
+            table.append(
+                (part.at[fields, pl.ds(0, count), rows], target.at[1, h], gx, me - 1, has_near, has_far)
+            )
 
     def copy(number):
         source, target, gx_to, depth_to = table[number][:4]
@@ -163,24 +192,17 @@
             device_id_type=MESH,
         )
 
-    for number in SEND_ORDER:
+    for number in range(len(table)):
         @pl.when(table[number][4])
         def _():
             copy(number).start()
 
-    def know():
-        for depth_to in (around(reach), around(-reach)):
-            pl.semaphore_signal(
-                known_sem.at[reach.bit_length() - 3], inc=1, device_id=(gx, depth_to), device_id_type=MESH
-            )
-
-    know()
     for _, target, _, _, _, comes in table:
         @pl.when(jnp.logical_not(comes))
         def _():
             target[...] = jnp.zeros(target.shape, F32)
 
-    for load in loads[3:]:
+    for load in loads[4:]:
         load.wait()
 
     step_len = 0.25 / cells_z
@@ -216,53 +238,56 @@
     keep_near = jnp.where(has_near, 1.0, 0.0).astype(F32)
     keep_far = jnp.where(has_far, 1.0, 0.0).astype(F32)
 
-    def filter_width(k, pair):
-        edge = jnp.concatenate([edge_in[0, k, pair], edge_in[1, k, pair]], axis=0)
-        if k != 1:
-            edge += jnp.concatenate(
-                [corner_in[k // 2, 0, pair], corner_in[k // 2, 1, pair]], axis=0
-            )
-        edge = jnp.transpose(jnp.concatenate([edge, jnp.zeros((112, 128), F32)], axis=0))
+    def turn_edges(k):
+        for pair in range(2):
+            edge = jnp.concatenate([edge_in[0, k, pair], edge_in[1, k, pair]], axis=0)
+            if k != 1:
+                edge += jnp.concatenate(
+                    [corner_in[k // 2, 0, pair], corner_in[k // 2, 1, pair]], axis=0
+                )
+            edge = jnp.transpose(jnp.concatenate([edge, jnp.zeros((112, 128), F32)], axis=0))
+            beside[k, pair, 0], beside[k, pair, 1] = halves(edge)
+
+    def filter_width(k, pair, start, size):
+        ys = slice(start, start + size)
+        edges = [
+            jnp.concatenate(
+                [beside[k, pair, i, 32 * j + start : 32 * j + start + size] for j in range(4)], axis=0
+            )
+            for i in range(2)
+        ]
         for f in range(2):
             field = 2 * pair + f
-            body = [part[field, 4 * k + j] for j in range(4)]
+            body = [part[field, 4 * k + j, ys] for j in range(4)]
             came, count = (z01_in, 3) if pair == 0 else (z23_in, 2)
             if k == 0:
                 for j in range(count):
-                    body[4 - count + j] += came[0, f, j]
+                    body[4 - count + j] += came[0, start // half, f, j]
             if k == 2:
                 for j in range(count):
-                    body[j] += came[1, f, j]
-            rows = jnp.concatenate(body, axis=0)
-            high, low = halves(jnp.concatenate([rows, edge], axis=1))
+                    body[j] += came[1, start // half, f, j]
+            own = halves(jnp.concatenate(body, axis=0))
+            high, low = [jnp.concatenate([own[i], edges[i]], axis=1) for i in range(2)]
+            weights = xw[f] if pair == 0 else xw[f, :, :width]
+            found = dot(high, weights) + dot(low, weights)
+            here = found[:, :width].reshape(4, size, width)
+            for j in range(4):
+                layer = here[j]
+                if pair == 0 and 4 * k + j == 1:
+                    layer = layer * keep_near
+                if pair == 0 and 4 * k + j == layers + 2:
+                    layer = layer * keep_far
+                smooth[field, 4 * k + j, 8 + start : 8 + start + size] = layer
             if pair == 0:
-                weights = xw[f]
-                found = dot(high, weights) + dot(low, weights)
-                here = found[:, :width].reshape(4, height, width)
-                for j in range(4):
-                    layer = here[j]
-                    if 4 * k + j == 1:
-                        layer = layer * keep_near
-                    if 4 * k + j == layers + 2:
-                        layer = layer * keep_far
-                    smooth[field, 4 * k + j, 8 : height + 8] = layer
-                slope[f, 4 * k : 4 * k + 4] = found[:, width:].reshape(4, height, width)
-            else:
-                weights = xw[f, :, :width]
-                found = dot(high, weights) + dot(low, weights)
-                smooth[field, 4 * k : 4 * k + 4, 8 : height + 8] = found.reshape(
-                    4, height, width
-                )
-
-    arrived(8, 9)
-    filter_width(1, 0)
-    filter_width(1, 1)
-    arrived(4, 5, 6, 7, 0, 1)
-    filter_width(0, 0)
-    filter_width(2, 0)
-    arrived(2, 3)
-    filter_width(0, 1)
-    filter_width(2, 1)
+                slope[f, 4 * k : 4 * k + 4, ys] = found[:, width:].reshape(4, size, width)
+
+    arrived(4, 5)
+    turn_edges(1)
+    filter_width(1, 0, 0, height)
+    filter_width(1, 1, 0, height)
+    arrived(0, 1, 2, 3)
+    turn_edges(0)
+    turn_edges(2)
 
     top = ext.shape[1] - 1
 
@@ -284,6 +309,13 @@
         )
 
     for t in range(height // 8):
+        if t < 2:
+            arrived(6 + 4 * t, 7 + 4 * t)
+            filter_width(0, 0, half * t, half)
+            filter_width(2, 0, half * t, half)
+            arrived(8 + 4 * t, 9 + 4 * t)
+            filter_width(0, 1, half * t, half)
+            filter_width(2, 1, half * t, half)
         here = pl.ds(8 * t + 8, 8)
         grads = []
         for f in range(2):
@@ -330,7 +362,7 @@
         for c in range(3):
             piece_out[pl.ds(8 * t, 8), c] = jnp.sum(weight * look(1 + c, at, fraction), axis=0)
         piece_out[pl.ds(8 * t, 8), 3] = opaque
-        if t == 0:
+        if t == 1:
             pl.semaphore_wait(known_sem.at[reach.bit_length() - 3], 2)
 
         @pl.loop(8 * t, 8 * t + 8)
@@ -384,7 +416,7 @@
         anywhere = pl.BlockSpec(memory_space=pl.ANY)
         image = pl.pallas_call(
             functools.partial(kernel, n_gx, n_depth, layers * n_depth),
-            out_shape=jax.ShapeDtypeStruct((4, width), F32),
+            out_shape=pltpu.VMEM((4, width), F32),
             in_specs=[anywhere] * 7,
             out_specs=pl.BlockSpec(memory_space=pltpu.VMEM),
             scratch_shapes=[
@@ -400,15 +432,16 @@
                 pltpu.VMEM((2, 3, 2, 8, 128), F32),
                 pltpu.VMEM((2, 3, 2, 8, 128), F32),
                 pltpu.VMEM((2, 2, 2, 8, 128), F32),
-                pltpu.VMEM((2, 2, 3, height, width), F32),
-                pltpu.VMEM((2, 2, 2, height, width), F32),
+                pltpu.VMEM((2, 2, 2, 3, height // 2, width), F32),
+                pltpu.VMEM((2, 2, 2, 2, height // 2, width), F32),
+                pltpu.VMEM((3, 2, 2, 128, 128), BF16),
                 pltpu.VMEM((fields, layers + 4, height + 16, width), F32),
                 pltpu.VMEM((2, layers + 4, height, width), F32),
                 pltpu.VMEM((n_depth, 4, width), F32),
                 pltpu.VMEM((n_depth, 4, width), F32),
-                pltpu.SemaphoreType.DMA((7,)),
-                pltpu.SemaphoreType.DMA((10,)),
-                pltpu.SemaphoreType.DMA((10,)),
+                pltpu.SemaphoreType.DMA((8,)),
+                pltpu.SemaphoreType.DMA((14,)),
+                pltpu.SemaphoreType.DMA((14,)),
                 pltpu.SemaphoreType.DMA,
                 pltpu.SemaphoreType.DMA,
                 pltpu.SemaphoreType.REGULAR((2,)),

time: 27.6 us -> 25.6 us (0.928)
  Pallas kernels: 26.2 us -> 24.8 us
  local copies, waits for them, and re-layouts: 1.26 us -> 0.58 us
    pallas_call x1, Pallas kernels: 26.2 us -> 24.8 us  [per_device(): pl.pallas_call(functools.partial(kernel, n_gx, n_depth, layers * n_depth)...]
    unnamed x1, local copies, waits for them, and re-layouts: 1.26 us -> 0.58 us
where the time goes in v3:
time: 25.6 us; the launch traced here: 25.4 us
  Pallas kernels  24.8 us (97%)
  local copies, waits for them, and re-layouts  0.58 us (2%)
    pallas_call x1, Pallas kernels, per_device(): pl.pallas_call(functools.partial(kernel, n_gx, n_depth, layers * n_depth)...  24.8 us
    unnamed x1, local copies, waits for them, and re-layouts  0.58 us

profile of v3, /device:TPU:25, one launch (start us, length us, event | category | flops | bytes accessed | tf_op | source)
XLA Modules:
  0.0 25.4 jit_solution(11053093089238726560)
XLA Ops:
  0.0 24.8 %shard_map.73 = f32[4,128]{1,0:T(4,128)S(1)} custom-call(f32[4,8,32,128]{3,2,1,0:T(8,128)} %vol_hbm.1, f32[1,128]{1,0:T(1,128)} %bitcast.8, f32[3,16]{1,0:T(4,128)} %bitcast.7, s32[1,128]{1,0:T(1,128)} %bitcast.9, bf16[384,256]{1,0:T(8,128)(2,1)} %constant.6.clone.zy_hbm, bf16[3,2,256,256]{3,2,1,0:T(8,128)(2,1)} %constant.7.clone.xw_hbm, ...), custom_call_target="tpu_custom_call" | custom-call | tf_op jit(solution)/shard_map/pallas_call | solution.py:417
  24.9 0.6 %copy.10 = f32[4,1,128]{2,1,0:T(1,128)} copy(f32[4,1,128]{2,1,0:T(1,128)S(1)} %bitcast.6) | data formatting | bytes 4096

commit v4 on v3

--- a/solution.py
+++ b/solution.py
@@ -104,7 +104,7 @@
         def _():
             pl.semaphore_signal(barrier, inc=1, device_id=(gx_to, depth_to), device_id_type=MESH)
 
-    for step, there in ((-1, has_near), (1, has_far), (0, True)):
+    for step, there in ((1, has_far), (0, True)):
         greet(gx - 1, me + step, has_left & there)
         greet(gx + 1, me + step, has_right & there)
     reach = 4
@@ -157,28 +157,22 @@
     loads[2].wait()
     filter_own(1)
     n_sides = has_left.astype(jnp.int32) + has_right.astype(jnp.int32)
-    n_rows = 1 + has_near.astype(jnp.int32) + has_far.astype(jnp.int32)
+    n_rows = 1 + has_near.astype(jnp.int32)
     pl.semaphore_wait(barrier, 2 * reach + n_sides * n_rows + n_first)
     know()
 
     table = [
-        (edge_out.at[0, 2], corner_in.at[0, 0], gx + 1, me + 1, has_right & has_far, has_left & has_near),
-        (edge_out.at[1, 2], corner_in.at[0, 1], gx - 1, me + 1, has_left & has_far, has_right & has_near),
-        (edge_out.at[0, 0], corner_in.at[1, 0], gx + 1, me - 1, has_right & has_near, has_left & has_far),
-        (edge_out.at[1, 0], corner_in.at[1, 1], gx - 1, me - 1, has_left & has_near, has_right & has_far),
+        (edge_out.at[0, pl.ds(0, 2)], corner_in.at[0], gx + 1, me - 1, has_right & has_near, has_left & has_far),
+        (edge_out.at[1, pl.ds(0, 2)], corner_in.at[1], gx - 1, me - 1, has_left & has_near, has_right & has_far),
         (edge_out.at[0], edge_in.at[0], gx + 1, me, has_right, has_left),
         (edge_out.at[1], edge_in.at[1], gx - 1, me, has_left, has_right),
     ]
     half = height // 2
     for h in range(2):
         rows = pl.ds(h * half, half)
-        for fields, count, target in ((pl.ds(0, 2), 3, z01_in), (pl.ds(2, 2), 2, z23_in)):
-            last = pl.ds(layers + 4 - count, count)
+        for fields, count, target in ((pl.ds(0, 2), 6, z01_in), (pl.ds(2, 2), 5, z23_in)):
             table.append(
-                (part.at[fields, last, rows], target.at[0, h], gx, me + 1, has_far, has_near)
-            )
-            table.append(
-                (part.at[fields, pl.ds(0, count), rows], target.at[1, h], gx, me - 1, has_near, has_far)
+                (part.at[fields, pl.ds(0, count), rows], target.at[h], gx, me - 1, has_near, has_far)
             )
 
     def copy(number):
@@ -219,7 +213,7 @@
     tab[0:4] = entries
     tab[4:8] = jnp.concatenate([entries[:, 1:], entries[:, :1]], axis=1) - entries
 
-    zeros8 = jnp.zeros((layers + 4, 8, width), F32)
+    zeros8 = jnp.zeros((layers + 8, 8, width), F32)
     for f in range(2):
         smooth[f, :, 0:8] = zeros8
         smooth[f, :, height + 8 : height + 16] = zeros8
@@ -240,63 +234,79 @@
 
     def turn_edges(k):
         for pair in range(2):
-            edge = jnp.concatenate([edge_in[0, k, pair], edge_in[1, k, pair]], axis=0)
-            if k != 1:
+            edge = jnp.zeros((16, 128), F32)
+            if k < 3:
+                edge += jnp.concatenate([edge_in[0, k, pair], edge_in[1, k, pair]], axis=0)
+            if k >= 2:
                 edge += jnp.concatenate(
-                    [corner_in[k // 2, 0, pair], corner_in[k // 2, 1, pair]], axis=0
+                    [corner_in[0, k - 2, pair], corner_in[1, k - 2, pair]], axis=0
                 )
             edge = jnp.transpose(jnp.concatenate([edge, jnp.zeros((112, 128), F32)], axis=0))
             beside[k, pair, 0], beside[k, pair, 1] = halves(edge)
 
-    def filter_width(k, pair, start, size):
+    def filter_width(ks, start, size):
         ys = slice(start, start + size)
+        blocks = [(k, pair) for k in ks for pair in range(2)]
         edges = [
             jnp.concatenate(
-                [beside[k, pair, i, 32 * j + start : 32 * j + start + size] for j in range(4)], axis=0
+                [
+                    beside[k, pair, i, 32 * j + start : 32 * j + start + size]
+                    for k, pair in blocks
+                    for j in range(4)
+                ],
+                axis=0,
             )
             for i in range(2)
         ]
         for f in range(2):
-            field = 2 * pair + f
-            body = [part[field, 4 * k + j, ys] for j in range(4)]
-            came, count = (z01_in, 3) if pair == 0 else (z23_in, 2)
-            if k == 0:
-                for j in range(count):
-                    body[4 - count + j] += came[0, start // half, f, j]
-            if k == 2:
-                for j in range(count):
-                    body[j] += came[1, start // half, f, j]
+            body = []
+            for k, pair in blocks:
+                came, count = (z01_in, 6) if pair == 0 else (z23_in, 5)
+                layer = []
+                for j in range(4):
+                    terms = []
+                    if 4 * k + j < layers + 4:
+                        terms.append(part[2 * pair + f, 4 * k + j, ys])
+                    if 0 <= 4 * k + j - layers < count:
+                        terms.append(came[start // half, f, 4 * k + j - layers])
+                    layer.append(sum(terms) if terms else jnp.zeros((size, width), F32))
+                body += layer
             own = halves(jnp.concatenate(body, axis=0))
-            high, low = [jnp.concatenate([own[i], edges[i]], axis=1) for i in range(2)]
-            weights = xw[f] if pair == 0 else xw[f, :, :width]
-            found = dot(high, weights) + dot(low, weights)
-            here = found[:, :width].reshape(4, size, width)
-            for j in range(4):
-                layer = here[j]
-                if pair == 0 and 4 * k + j == 1:
-                    layer = layer * keep_near
-                if pair == 0 and 4 * k + j == layers + 2:
-                    layer = layer * keep_far
-                smooth[field, 4 * k + j, 8 + start : 8 + start + size] = layer
-            if pair == 0:
-                slope[f, 4 * k : 4 * k + 4, ys] = found[:, width:].reshape(4, size, width)
-
-    arrived(4, 5)
+            both = jnp.concatenate(
+                [jnp.concatenate([own[i], edges[i]], axis=1) for i in range(2)], axis=0
+            )
+            found = dot(both, xw[f])
+            found = found[: found.shape[0] // 2] + found[found.shape[0] // 2 :]
+            for at, (k, pair) in enumerate(blocks):
+                here = found[4 * size * at : 4 * size * (at + 1)]
+                if pair == 0:
+                    slope[f, 4 * k : 4 * k + 4, ys] = here[:, width:].reshape(4, size, width)
+                here = here[:, :width].reshape(4, size, width)
+                for j in range(4):
+                    layer = here[j]
+                    if pair == 0 and 4 * k + j == 1:
+                        layer = layer * keep_near
+                    if pair == 0 and 4 * k + j == layers + 2:
+                        layer = layer * keep_far
+                    smooth[2 * pair + f, 4 * k + j, 8 + start : 8 + start + size] = layer
+
+    arrived(2, 3)
+    turn_edges(0)
     turn_edges(1)
-    filter_width(1, 0, 0, height)
-    filter_width(1, 1, 0, height)
-    arrived(0, 1, 2, 3)
-    turn_edges(0)
+    filter_width((0, 1), 0, height)
+    arrived(0, 1)
     turn_edges(2)
-
+    turn_edges(3)
+
+    count = layers + 3
     top = ext.shape[1] - 1
 
     def look(row, at, fraction):
         def pick(r):
-            entry = jnp.broadcast_to(tab[r : r + 1], (layers * 8, 128))
+            entry = jnp.broadcast_to(tab[r : r + 1], (count * 8, 128))
             return jnp.take_along_axis(entry, at, axis=1, mode="promise_in_bounds")
 
-        return (pick(row) + fraction * pick(row + 4)).reshape(layers, 8, width)
+        return (pick(row) + fraction * pick(row + 4)).reshape(count, 8, width)
 
     def piece(to):
         return pltpu.make_async_remote_copy(
@@ -310,24 +320,20 @@
 
     for t in range(height // 8):
         if t < 2:
-            arrived(6 + 4 * t, 7 + 4 * t)
-            filter_width(0, 0, half * t, half)
-            filter_width(2, 0, half * t, half)
-            arrived(8 + 4 * t, 9 + 4 * t)
-            filter_width(0, 1, half * t, half)
-            filter_width(2, 1, half * t, half)
+            arrived(4 + 2 * t, 5 + 2 * t)
+            filter_width((2, 3), half * t, half)
         here = pl.ds(8 * t + 8, 8)
         grads = []
         for f in range(2):
             grads.append(
                 (
-                    0.5 * (smooth[f, 3 : layers + 3, here] - smooth[f, 1 : layers + 1, here]),
+                    0.5 * (smooth[f, 3 : count + 3, here] - smooth[f, 1 : count + 1, here]),
                     0.5
                     * (
-                        smooth[f, 2 : layers + 2, 8 * t + 9 : 8 * t + 17]
-                        - smooth[f, 2 : layers + 2, 8 * t + 7 : 8 * t + 15]
+                        smooth[f, 2 : count + 2, 8 * t + 9 : 8 * t + 17]
+                        - smooth[f, 2 : count + 2, 8 * t + 7 : 8 * t + 15]
                     ),
-                    slope[f, 2 : layers + 2, pl.ds(8 * t, 8)],
+                    slope[f, 2 : count + 2, pl.ds(8 * t, 8)],
                 )
             )
         z0, y0, x0 = grads[0]
@@ -337,14 +343,14 @@
         shading = 0.35 + 0.65 * facing * facing / (steep + 0.05)
         warm = z1 * z1 + y1 * y1 + x1 * x1
         gain = 0.25 + 1.5 * warm / (warm + 0.1)
-        place = (0.5 * top) * (1.0 + jnp.tanh(smooth[0, 2 : layers + 2, here]))
+        place = (0.5 * top) * (1.0 + jnp.tanh(smooth[0, 2 : count + 2, here]))
         at = jnp.clip(place.astype(jnp.int32), 0, top - 1)
-        fraction = (place - at.astype(F32)).reshape(layers * 8, width)
-        at = at.reshape(layers * 8, width)
+        fraction = (place - at.astype(F32)).reshape(count * 8, width)
+        at = at.reshape(count * 8, width)
         tau = look(0, at, fraction) * gain
         bright = (
-            (1.0 + 0.5 * jnp.tanh(smooth[2, 2 : layers + 2, here]))
-            * jnp.exp(0.5 * jnp.tanh(smooth[3, 2 : layers + 2, here]))
+            (1.0 + 0.5 * jnp.tanh(smooth[2, 2 : count + 2, here]))
+            * jnp.exp(0.5 * jnp.tanh(smooth[3, 2 : count + 2, here]))
             * shading
         )
         absorbed = tau * (
@@ -354,8 +360,13 @@
         )
         opaque = jnp.zeros((8, width), F32)
         weights = []
-        for z in range(layers):
-            weight = absorbed[z] - absorbed[z] * opaque
+        for z in range(count):
+            here = absorbed[z]
+            if z < 3:
+                here = here * (1.0 - keep_near)
+            if z >= layers:
+                here = here * keep_far
+            weight = here - here * opaque
             weights.append(weight[None])
             opaque = opaque + weight
         weight = jnp.concatenate(weights, axis=0) * bright
@@ -432,16 +443,16 @@
                 pltpu.VMEM((2, 3, 2, 8, 128), F32),
                 pltpu.VMEM((2, 3, 2, 8, 128), F32),
                 pltpu.VMEM((2, 2, 2, 8, 128), F32),
-                pltpu.VMEM((2, 2, 2, 3, height // 2, width), F32),
-                pltpu.VMEM((2, 2, 2, 2, height // 2, width), F32),
-                pltpu.VMEM((3, 2, 2, 128, 128), BF16),
-                pltpu.VMEM((fields, layers + 4, height + 16, width), F32),
-                pltpu.VMEM((2, layers + 4, height, width), F32),
+                pltpu.VMEM((2, 2, 6, height // 2, width), F32),
+                pltpu.VMEM((2, 2, 5, height // 2, width), F32),
+                pltpu.VMEM((4, 2, 2, 128, 128), BF16),
+                pltpu.VMEM((fields, layers + 8, height + 16, width), F32),
+                pltpu.VMEM((2, layers + 8, height, width), F32),
                 pltpu.VMEM((n_depth, 4, width), F32),
                 pltpu.VMEM((n_depth, 4, width), F32),
                 pltpu.SemaphoreType.DMA((8,)),
-                pltpu.SemaphoreType.DMA((14,)),
-                pltpu.SemaphoreType.DMA((14,)),
+                pltpu.SemaphoreType.DMA((8,)),
+                pltpu.SemaphoreType.DMA((8,)),
                 pltpu.SemaphoreType.DMA,
                 pltpu.SemaphoreType.DMA,
                 pltpu.SemaphoreType.REGULAR((2,)),

time: 25.6 us -> 25.3 us (0.988)
  no operation moved by 1% of the time
where the time goes in v4:
time: 25.3 us; the launch traced here: 25.2 us
  Pallas kernels  24.6 us (97%)
  local copies, waits for them, and re-layouts  0.58 us (2%)
    pallas_call x1, Pallas kernels, per_device(): pl.pallas_call(functools.partial(kernel, n_gx, n_depth, layers * n_depth)...  24.6 us
    unnamed x1, local copies, waits for them, and re-layouts  0.58 us

profile of v4, /device:TPU:25, one launch (start us, length us, event | category | flops | bytes accessed | tf_op | source)
XLA Modules:
  0.0 25.2 jit_solution(1574115949515072765)
XLA Ops:
  0.0 24.6 %shard_map.73 = f32[4,128]{1,0:T(4,128)S(1)} custom-call(f32[4,8,32,128]{3,2,1,0:T(8,128)} %vol_hbm.1, f32[1,128]{1,0:T(1,128)} %bitcast.8, f32[3,16]{1,0:T(4,128)} %bitcast.7, s32[1,128]{1,0:T(1,128)} %bitcast.9, bf16[384,256]{1,0:T(8,128)(2,1)} %constant.6.clone.zy_hbm, bf16[3,2,256,256]{3,2,1,0:T(8,128)(2,1)} %constant.7.clone.xw_hbm, ...), custom_call_target="tpu_custom_call" | custom-call | tf_op jit(solution)/shard_map/pallas_call | solution.py:428
  24.6 0.6 %copy.10 = f32[4,1,128]{2,1,0:T(1,128)} copy(f32[4,1,128]{2,1,0:T(1,128)S(1)} %bitcast.6) | data formatting | bytes 4096

commit v5 on v4

--- a/solution.py
+++ b/solution.py
@@ -293,7 +293,7 @@
     arrived(2, 3)
     turn_edges(0)
     turn_edges(1)
-    filter_width((0, 1), 0, height)
+    filter_width((0, 1), 0, half)
     arrived(0, 1)
     turn_edges(2)
     turn_edges(3)
@@ -321,7 +321,7 @@
     for t in range(height // 8):
         if t < 2:
             arrived(4 + 2 * t, 5 + 2 * t)
-            filter_width((2, 3), half * t, half)
+            filter_width((2, 3) if t == 0 else (0, 1, 2, 3), half * t, half)
         here = pl.ds(8 * t + 8, 8)
         grads = []
         for f in range(2):

time: 25.3 us -> 25.2 us (level)
  no operation moved by 1% of the time
where the time goes in v5:
time: 25.2 us; the launch traced here: 25.1 us
  Pallas kernels  24.5 us (97%)
  local copies, waits for them, and re-layouts  0.58 us (2%)
    pallas_call x1, Pallas kernels, per_device(): pl.pallas_call(functools.partial(kernel, n_gx, n_depth, layers * n_depth)...  24.5 us
    unnamed x1, local copies, waits for them, and re-layouts  0.58 us

profile of v5, /device:TPU:25, one launch (start us, length us, event | category | flops | bytes accessed | tf_op | source)
XLA Modules:
  0.0 25.1 jit_solution(8393528492733324321)
XLA Ops:
  0.0 24.5 %shard_map.73 = f32[4,128]{1,0:T(4,128)S(1)} custom-call(f32[4,8,32,128]{3,2,1,0:T(8,128)} %vol_hbm.1, f32[1,128]{1,0:T(1,128)} %bitcast.8, f32[3,16]{1,0:T(4,128)} %bitcast.7, s32[1,128]{1,0:T(1,128)} %bitcast.9, bf16[384,256]{1,0:T(8,128)(2,1)} %constant.6.clone.zy_hbm, bf16[3,2,256,256]{3,2,1,0:T(8,128)(2,1)} %constant.7.clone.xw_hbm, ...), custom_call_target="tpu_custom_call" | custom-call | tf_op jit(solution)/shard_map/pallas_call | solution.py:428
  24.5 0.6 %copy.10 = f32[4,1,128]{2,1,0:T(1,128)} copy(f32[4,1,128]{2,1,0:T(1,128)S(1)} %bitcast.6) | data formatting | bytes 4096

commit v6 on v5

--- a/solution.py
+++ b/solution.py
@@ -290,13 +290,9 @@
                         layer = layer * keep_far
                     smooth[2 * pair + f, 4 * k + j, 8 + start : 8 + start + size] = layer
 
-    arrived(2, 3)
-    turn_edges(0)
-    turn_edges(1)
-    filter_width((0, 1), 0, half)
-    arrived(0, 1)
-    turn_edges(2)
-    turn_edges(3)
+    arrived(0, 1, 4, 5, 2, 3)
+    for k in range(4):
+        turn_edges(k)
 
     count = layers + 3
     top = ext.shape[1] - 1
@@ -320,8 +316,9 @@
 
     for t in range(height // 8):
         if t < 2:
-            arrived(4 + 2 * t, 5 + 2 * t)
-            filter_width((2, 3) if t == 0 else (0, 1, 2, 3), half * t, half)
+            if t == 1:
+                arrived(6, 7)
+            filter_width((0, 1, 2, 3), half * t, half)
         here = pl.ds(8 * t + 8, 8)
         grads = []
         for f in range(2):

time: 25.2 us -> 25 us (level)
  no operation moved by 1% of the time
where the time goes in v6:
time: 25 us; the launch traced here: 24.9 us
  Pallas kernels  24.3 us (97%)
  local copies, waits for them, and re-layouts  0.58 us (2%)
    pallas_call x1, Pallas kernels, per_device(): pl.pallas_call(functools.partial(kernel, n_gx, n_depth, layers * n_depth)...  24.3 us
    unnamed x1, local copies, waits for them, and re-layouts  0.58 us

profile of v6, /device:TPU:25, one launch (start us, length us, event | category | flops | bytes accessed | tf_op | source)
XLA Modules:
  0.0 24.9 jit_solution(340590541689721525)
XLA Ops:
  0.0 24.3 %shard_map.73 = f32[4,128]{1,0:T(4,128)S(1)} custom-call(f32[4,8,32,128]{3,2,1,0:T(8,128)} %vol_hbm.1, f32[1,128]{1,0:T(1,128)} %bitcast.8, f32[3,16]{1,0:T(4,128)} %bitcast.7, s32[1,128]{1,0:T(1,128)} %bitcast.9, bf16[384,256]{1,0:T(8,128)(2,1)} %constant.6.clone.zy_hbm, bf16[3,2,256,256]{3,2,1,0:T(8,128)(2,1)} %constant.7.clone.xw_hbm, ...), custom_call_target="tpu_custom_call" | custom-call | tf_op jit(solution)/shard_map/pallas_call | solution.py:425
  24.3 0.6 %copy.10 = f32[4,1,128]{2,1,0:T(1,128)} copy(f32[4,1,128]{2,1,0:T(1,128)S(1)} %bitcast.6) | data formatting | bytes 4096

commit v7 on v6

--- a/solution.py
+++ b/solution.py
@@ -161,18 +161,20 @@
     pl.semaphore_wait(barrier, 2 * reach + n_sides * n_rows + n_first)
     know()
 
+    left, right = lax.rem(gx + n_gx - 1, n_gx), lax.rem(gx + 1, n_gx)
+    before = around(-1)
     table = [
-        (edge_out.at[0, pl.ds(0, 2)], corner_in.at[0], gx + 1, me - 1, has_right & has_near, has_left & has_far),
-        (edge_out.at[1, pl.ds(0, 2)], corner_in.at[1], gx - 1, me - 1, has_left & has_near, has_right & has_far),
-        (edge_out.at[0], edge_in.at[0], gx + 1, me, has_right, has_left),
-        (edge_out.at[1], edge_in.at[1], gx - 1, me, has_left, has_right),
+        (edge_out.at[0, pl.ds(0, 2)], corner_in.at[0], right, before, has_right & has_near, has_left & has_far),
+        (edge_out.at[1, pl.ds(0, 2)], corner_in.at[1], left, before, has_left & has_near, has_right & has_far),
+        (edge_out.at[0], edge_in.at[0], right, me, has_right, has_left),
+        (edge_out.at[1], edge_in.at[1], left, me, has_left, has_right),
     ]
     half = height // 2
     for h in range(2):
         rows = pl.ds(h * half, half)
         for fields, count, target in ((pl.ds(0, 2), 6, z01_in), (pl.ds(2, 2), 5, z23_in)):
             table.append(
-                (part.at[fields, pl.ds(0, count), rows], target.at[h], gx, me - 1, has_near, has_far)
+                (part.at[fields, pl.ds(0, count), rows], target.at[h], gx, before, has_near, has_far)
             )
 
     def copy(number):

time: 25 us -> 25 us (level)
  no operation moved by 1% of the time
where the time goes in v7:
time: 25 us; the launch traced here: 24.9 us
  Pallas kernels  24.3 us (97%)
  local copies, waits for them, and re-layouts  0.58 us (2%)
    pallas_call x1, Pallas kernels, per_device(): pl.pallas_call(functools.partial(kernel, n_gx, n_depth, layers * n_depth)...  24.3 us
    unnamed x1, local copies, waits for them, and re-layouts  0.58 us

profile of v7, /device:TPU:25, one launch (start us, length us, event | category | flops | bytes accessed | tf_op | source)
XLA Modules:
  0.0 24.9 jit_solution(15681708550921923454)
XLA Ops:
  0.0 24.3 %shard_map.73 = f32[4,128]{1,0:T(4,128)S(1)} custom-call(f32[4,8,32,128]{3,2,1,0:T(8,128)} %vol_hbm.1, f32[1,128]{1,0:T(1,128)} %bitcast.8, f32[3,16]{1,0:T(4,128)} %bitcast.7, s32[1,128]{1,0:T(1,128)} %bitcast.9, bf16[384,256]{1,0:T(8,128)(2,1)} %constant.6.clone.zy_hbm, bf16[3,2,256,256]{3,2,1,0:T(8,128)(2,1)} %constant.7.clone.xw_hbm, ...), custom_call_target="tpu_custom_call" | custom-call | tf_op jit(solution)/shard_map/pallas_call | solution.py:427
  24.3 0.6 %copy.10 = f32[4,1,128]{2,1,0:T(1,128)} copy(f32[4,1,128]{2,1,0:T(1,128)S(1)} %bitcast.6) | data formatting | bytes 4096
